TPU v7x, 256 devices: a whole 4x4x8 slice. The times are simulated.
256 devices in a mesh: gx: 16 (over x, z_hi), gy: 16 (over z_lo, y, core).
Axes of the slice: x: 4, y: 4, z: 8 (z_hi: 4, z_lo: 2; z = z_hi * 2 + z_lo), core: 2. Of those that a mesh axis runs over, the one named last changes fastest.
Arguments:
- phase_start: float32 [384, 256, 256], P('gx', 'gy'), may hold values from 0 to 1
- potential_start: float32 [384, 256, 256], P('gx', 'gy'), may hold values from -6 to 6
- phase_cotangent: float32 [384, 256, 256], P('gx', 'gy'), may hold values from -6 to 6
- potential_cotangent: float32 [384, 256, 256], P('gx', 'gy'), may hold values from -6 to 6
- orientation: int32 [384, 256, 256], P('gx', 'gy'), may hold values from 0 to 7
- anisotropy_index: int32 [384, 256, 256], P('gx', 'gy'), may hold values from 0 to 15
- boundary_mask: int32 [384, 256, 256], P('gx', 'gy'), may hold values 0 or 1
- stiffness_table: float32 [16], replicated, may hold values from 0.2 to 1.2
- partition_table: float32 [8], replicated, may hold values from 0.1 to 0.9
Outputs:
- phase_gradient: float32 [384, 256, 256], P('gx', 'gy')
- potential_gradient: float32 [384, 256, 256], P('gx', 'gy')
All inputs are finite; a program needn't handle non-finite values. No bound on the sum of `boundary_mask` on one device may be relied on, other than what follows from the above.
Results may differ from a plain program's by a relative error of at most 0.000062.
Values sent between devices are 32-bit elements; how exact they have to be, the bound alone decides.
A program may use at most 64 MiB of HBM per device.

v0:
```python
import jax
import jax.numpy as jnp
from jax import lax
from jax.sharding import PartitionSpec as P

mobility_step = 0.1
well_height = 1.0
coupling = 1.0
diffusion_step = 0.03


def extended(shard, sides, width):
    for axis, dim in sides:
        size, length = (lax.axis_size(axis), shard.shape[dim])
        up = [(i, (i + 1) % size) for i in range(size - 1)]
        down = [(j, i) for i, j in up]
        last = lax.slice_in_dim(shard, length - width, length, axis=dim)
        leading = lax.slice_in_dim(shard, 0, width, axis=dim)
        before = lax.ppermute(last, axis, up)
        after = lax.ppermute(leading, axis, down)
        shard = jnp.concatenate([before, shard, after], axis=dim)
    return shard


def passed_along(shard, axis, by):
    size = lax.axis_size(axis)
    pairs = [(i, i + by) for i in range(size) if 0 <= i + by < size]
    return lax.ppermute(shard, axis, pairs)


def lookup(indices, table):
    classes = jnp.arange(table.shape[0], dtype=jnp.int32)
    picked = jnp.where(
        indices[None] == classes[:, None, None, None], table[:, None, None, None], jnp.float32(0.0)
    )
    return jnp.sum(picked, axis=0)


def lap_padded(padded):
    center = padded[:, 1:-1, 1:-1, :]
    beside = padded[:, 2:, 1:-1, :] + padded[:, :-2, 1:-1, :]
    beside = beside + padded[:, 1:-1, 2:, :] + padded[:, 1:-1, :-2, :]
    zwide = jnp.pad(center, ((0, 0), (0, 0), (0, 0), (1, 1)))
    beside = beside + zwide[..., 2:] + zwide[..., :-2]
    return beside - 6.0 * center


def reaction(state, laps, stiffness, jump, movable):
    phase = state[0]
    potential = state[1]
    denominator = phase * phase + (1.0 - phase) * (1.0 - phase)
    interp = phase * phase / denominator
    slope = 2.0 * phase * (1.0 - phase) / (denominator * denominator)
    drive = (
        stiffness * laps[0]
        - 2.0 * well_height * phase * (1.0 - phase) * (1.0 - 2.0 * phase)
        + coupling * jump * slope * potential
    )
    phase_next = phase + movable * mobility_step * drive
    potential_next = potential + movable * (
        diffusion_step * laps[1] - jump * slope * (phase_next - phase)
    ) / (1.0 - jump * interp)
    return jnp.stack([phase_next, potential_next])


def extend_state(state):
    return extended(state, (("gx", 1), ("gy", 2)), 1)


def on_device(
    phase_start,
    potential_start,
    phase_cotangent,
    potential_cotangent,
    orientation,
    anisotropy_index,
    boundary_mask,
    stiffness_table,
    partition_table,
):
    stiffness = lookup(anisotropy_index, stiffness_table)
    jump = 1.0 - lookup(orientation, partition_table)
    movable = 1.0 - boundary_mask.astype(jnp.float32)

    def advance(padded):
        return reaction(padded[:, 1:-1, 1:-1, :], lap_padded(padded), stiffness, jump, movable)

    state_zero = jnp.stack([phase_start, potential_start])
    padded_zero = extend_state(state_zero)
    state_one = advance(padded_zero)
    padded_one = extend_state(state_one)
    cotangent = jnp.stack([phase_cotangent, potential_cotangent])
    for padded in (padded_one, padded_zero):
        outputs, pullback = jax.vjp(advance, padded)
        wide_cotangent = pullback(cotangent)[0]
        interior = wide_cotangent[:, 1:-1, 1:-1, :]
        from_above = passed_along(wide_cotangent[:, 0, 1:-1, :], "gx", -1)
        from_below = passed_along(wide_cotangent[:, -1, 1:-1, :], "gx", 1)
        interior = interior.at[:, -1, :, :].add(from_above)
        interior = interior.at[:, 0, :, :].add(from_below)
        from_right = passed_along(wide_cotangent[:, 1:-1, 0, :], "gy", -1)
        from_left = passed_along(wide_cotangent[:, 1:-1, -1, :], "gy", 1)
        interior = interior.at[:, :, -1, :].add(from_right)
        interior = interior.at[:, :, 0, :].add(from_left)
        cotangent = interior
    return (cotangent[0], cotangent[1])


def solution(mesh):
    in_specs = (
        P("gx", "gy", None),
        P("gx", "gy", None),
        P("gx", "gy", None),
        P("gx", "gy", None),
        P("gx", "gy", None),
        P("gx", "gy", None),
        P("gx", "gy", None),
        P(),
        P(),
    )
    out_specs = (P("gx", "gy", None), P("gx", "gy", None))
    return jax.shard_map(
        on_device, mesh=mesh, in_specs=in_specs, out_specs=out_specs, check_vma=False
    )
```

profile of v0, /device:TPU:34, one launch (start us, length us, event | category | flops | bytes accessed | tf_op | source)
XLA Modules:
  0.0 110.3 jit_solution(16461271187977027575)
XLA Ops:
  0.7 1.6 %copy_bitcast_fusion.1 = (f32[1,24,16,256]{3,1,2,0:T(8,128)S(1)}, f32[1,24,16,256]{3,1,2,0:T(8,128)S(1)}) fusion(f32[24,16,256]{2,1,0:T(8,128)} %param.26, f32[24,16,256]{2,1,0:T(8,128)} %param.25), kind=kLoop, calls=%fused_computation.165 | loop fusion | bytes 1572864 | tf_op jit(solution)/shard_map/stack | solution.py:88
  2.4 5.2 %collective-permute-start.1 = (f32[2,1,16,256]{3,1,2,0:T(1,128)S(1)}, f32[2,1,16,256]{3,1,2,0:T(1,128)S(1)}, u32[]{:S(2)}, u32[]{:S(2)}) collective-permute-start(f32[2,1,16,256]{3,1,2,0:T(1,128)S(1)} %get-tuple-element.145), channel_id=1, source_target_pairs={{0,16},{16,32},{32,48},{48,64},{64,80},{80,96},{96,112},{112,128},... | collective-permute-start | bytes 98312 | tf_op jit(solution)/shard_map/ppermute | solution.py:19
  7.6 4.0 %collective-permute-start = (f32[2,1,16,256]{3,1,2,0:T(1,128)S(1)}, f32[2,1,16,256]{3,1,2,0:T(1,128)S(1)}, u32[]{:S(2)}, u32[]{:S(2)}) collective-permute-start(f32[2,1,16,256]{3,1,2,0:T(1,128)S(1)} %get-tuple-element.146), channel_id=1, source_target_pairs={{16,0},{32,16},{48,32},{64,48},{80,64},{96,80},{112,96},{128,112},... | collective-permute-start | bytes 98312 | tf_op jit(solution)/shard_map/ppermute | solution.py:20
  11.6 0.7 select_reduce_fusion
  12.3 0.4 select_reduce_fusion.1
  12.8 2.2 %collective-permute-done = f32[2,1,16,256]{3,1,2,0:T(1,128)S(1)} collective-permute-done((f32[2,1,16,256]{3,1,2,0:T(1,128)S(1)}, f32[2,1,16,256]{3,1,2,0:T(1,128)S(1)}, u32[]{:S(2)}, u32[]{:S(2)}) %collective-permute-start) | collective-permute-done | bytes 32800 | tf_op jit(solution)/shard_map/ppermute | solution.py:20
  15.0 3.7 %collective-permute-start.2 = (f32[2,26,1,256]{3,1,2,0:T(8,128)S(1)}, f32[2,26,1,256]{3,1,2,0:T(8,128)S(1)}, u32[]{:S(2)}, u32[]{:S(2)}) collective-permute-start(f32[2,26,1,256]{3,1,2,0:T(8,128)S(1)} %get-tuple-element.138), channel_id=1, source_target_pairs={{1,0},{2,1},{3,2},{4,3},{5,4},{6,5},{7,6},{8,7},{9,8},{10,9},{11,1... | collective-permute-start | bytes 159752 | tf_op jit(solution)/shard_map/ppermute | solution.py:20
  18.6 1.9 %collective-permute-start.3 = (f32[2,26,1,256]{3,1,2,0:T(8,128)S(1)}, f32[2,26,1,256]{3,1,2,0:T(8,128)S(1)}, u32[]{:S(2)}, u32[]{:S(2)}) collective-permute-start(f32[2,26,1,256]{3,1,2,0:T(8,128)S(1)} %get-tuple-element.139), channel_id=1, source_target_pairs={{0,1},{1,2},{2,3},{3,4},{4,5},{5,6},{6,7},{7,8},{8,9},{9,10},{10,1... | collective-permute-start | bytes 159752 | tf_op jit(solution)/shard_map/ppermute | solution.py:19
  20.7 5.7 %collective-permute-done.3 = f32[2,26,1,256]{3,1,2,0:T(8,128)S(1)} collective-permute-done((f32[2,26,1,256]{3,1,2,0:T(8,128)S(1)}, f32[2,26,1,256]{3,1,2,0:T(8,128)S(1)}, u32[]{:S(2)}, u32[]{:S(2)}) %collective-permute-start.3) | collective-permute-done | bytes 53280 | tf_op jit(solution)/shard_map/ppermute | solution.py:19
  26.3 0.6 fusion.2
  27.0 1.2 %multiply_divide_fusion.1 = (f32[24,16,256]{2,0,1:T(8,128)S(1)}, f32[24,16,256]{2,0,1:T(8,128)S(1)}, f32[24,16,256]{2,0,1:T(8,128)S(1)}) fusion(f32[24,16,256]{2,1,0:T(8,128)S(1)} %copy-done.2, f32[24,16,256]{2,1,0:T(8,128)S(1)} %broadcast_subtract_fusion, f32[2,24,16,256]{3,1,2,0:T(8,128)S(1)} %fusion.2, f32[24,16,256]{2,1,0:T(8,128)S(1)} %select_reduce_fusion, ...), kind=kLoop, calls=%fused_computation.166 | loop fusion | flops 2555904 | bytes 3538944 | tf_op jit(solution)/shard_map/jvp()/div | solution.py:52
  28.2 1.0 divide_add_fusion
  29.2 5.8 %collective-permute-start.5 = (f32[2,1,16,256]{3,1,2,0:T(1,128)S(1)}, f32[2,1,16,256]{3,1,2,0:T(1,128)S(1)}, u32[]{:S(2)}, u32[]{:S(2)}) collective-permute-start(f32[2,1,16,256]{3,1,2,0:T(1,128)S(1)} %get-tuple-element.143), channel_id=1, source_target_pairs={{0,16},{16,32},{32,48},{48,64},{64,80},{80,96},{96,112},{112,128},... | collective-permute-start | bytes 98312 | tf_op jit(solution)/shard_map/ppermute | solution.py:19
  35.0 3.1 %collective-permute-start.4 = (f32[2,1,16,256]{3,1,2,0:T(1,128)S(1)}, f32[2,1,16,256]{3,1,2,0:T(1,128)S(1)}, u32[]{:S(2)}, u32[]{:S(2)}) collective-permute-start(f32[2,1,16,256]{3,1,2,0:T(1,128)S(1)} %get-tuple-element.144), channel_id=1, source_target_pairs={{16,0},{32,16},{48,32},{64,48},{80,64},{96,80},{112,96},{128,112},... | collective-permute-start | bytes 98312 | tf_op jit(solution)/shard_map/ppermute | solution.py:20
  38.1 3.6 %collective-permute-done.4 = f32[2,1,16,256]{3,1,2,0:T(1,128)S(1)} collective-permute-done((f32[2,1,16,256]{3,1,2,0:T(1,128)S(1)}, f32[2,1,16,256]{3,1,2,0:T(1,128)S(1)}, u32[]{:S(2)}, u32[]{:S(2)}) %collective-permute-start.4) | collective-permute-done | bytes 32800 | tf_op jit(solution)/shard_map/ppermute | solution.py:20
  41.7 1.9 %collective-permute-start.6 = (f32[2,26,1,256]{3,1,2,0:T(8,128)S(1)}, f32[2,26,1,256]{3,1,2,0:T(8,128)S(1)}, u32[]{:S(2)}, u32[]{:S(2)}) collective-permute-start(f32[2,26,1,256]{3,1,2,0:T(8,128)S(1)} %get-tuple-element.136), channel_id=1, source_target_pairs={{1,0},{2,1},{3,2},{4,3},{5,4},{6,5},{7,6},{8,7},{9,8},{10,9},{11,1... | collective-permute-start | bytes 159752 | tf_op jit(solution)/shard_map/ppermute | solution.py:20
  43.7 2.6 %collective-permute-start.7 = (f32[2,26,1,256]{3,1,2,0:T(8,128)S(1)}, f32[2,26,1,256]{3,1,2,0:T(8,128)S(1)}, u32[]{:S(2)}, u32[]{:S(2)}) collective-permute-start(f32[2,26,1,256]{3,1,2,0:T(8,128)S(1)} %get-tuple-element.137), channel_id=1, source_target_pairs={{0,1},{1,2},{2,3},{3,4},{4,5},{5,6},{6,7},{7,8},{8,9},{9,10},{10,1... | collective-permute-start | bytes 159752 | tf_op jit(solution)/shard_map/ppermute | solution.py:19
  46.3 5.0 %collective-permute-done.7 = f32[2,26,1,256]{3,1,2,0:T(8,128)S(1)} collective-permute-done((f32[2,26,1,256]{3,1,2,0:T(8,128)S(1)}, f32[2,26,1,256]{3,1,2,0:T(8,128)S(1)}, u32[]{:S(2)}, u32[]{:S(2)}) %collective-permute-start.7) | collective-permute-done | bytes 53280 | tf_op jit(solution)/shard_map/ppermute | solution.py:19
  51.4 0.5 fusion.4
  51.9 0.5 copy_subtract_fusion
  52.5 0.4 copy-done.4
  53.0 1.7 %add_multiply_fusion = (f32[24,16,256]{2,0,1:T(8,128)S(1)}, f32[24,16,256]{2,0,1:T(8,128)S(1)}, f32[24,16,256]{2,0,1:T(8,128)S(1)}, f32[24,16,256]{2,0,1:T(8,128...) fusion(f32[24,16,256]{2,0,1:T(8,128)S(1)} %get-tuple-element.113, ...), kind=kLoop, calls=%fused_computation.124 | loop fusion | flops 4423680 | bytes 5898240 | tf_op jit(solution)/shard_map/transpose(jvp())/add_any | solution.py:53
  54.7 0.9 copy_multiply_fusion.6
  55.6 1.9 %fusion.13 = (f32[24,16,256]{2,0,1:T(8,128)S(1)}, f32[1,24,16,256]{3,1,2,0:T(8,128)S(1)}, f32[1,24,16,256]{3,1,2,0:T(8,128)S(1)}, f32[1,24,16,256]{3,1,2,0:T(8,128)S(1)}) fusion(f32[24,16,256]{2,1,0:T(8,128)S(1)} %get-tuple-element.109, f32[24,16,256]{2,1,0:T(8,128)S(1)} %get-tuple-element.110, f32[24,16,256]{2,0,1:T(8,128)S(1)} %get-tuple-element.113, ...), kind=kLoop, calls=%fused_computation.71 | loop fusion | flops 4620288 | bytes 5898240 | tf_op jit(solution)/shard_map/transpose(jvp())/add_any | solution.py:51
  57.5 0.2 fusion.36
  57.7 0.1 copy.127
  57.9 0.5 fusion.9
  58.3 0.3 pad_add_fusion.1
  58.7 0.8 copy_add_fusion
  59.6 5.2 %collective-permute-start.8 = (f32[2,16,256]{2,0,1:T(2,128)S(1)}, f32[2,16,256]{2,0,1:T(2,128)S(1)}, u32[]{:S(2)}, u32[]{:S(2)}) collective-permute-start(f32[2,16,256]{2,0,1:T(2,128)S(1)} %bitcast.147), channel_id=1, source_target_pairs={{16,0},{32,16},{48,32},{64,48},{80,64},{96,80},{112,96},{128,112},... | collective-permute-start | bytes 98312 | tf_op jit(solution)/shard_map/ppermute | solution.py:28
  65.0 0.6 copy.377
  65.6 1.9 %collective-permute-start.9 = (f32[2,16,256]{2,0,1:T(2,128)}, f32[2,16,256]{2,0,1:T(2,128)}, u32[]{:S(2)}, u32[]{:S(2)}) collective-permute-start(f32[2,16,256]{2,0,1:T(2,128)} %bitcast.133), channel_id=1, source_target_pairs={{0,16},{16,32},{32,48},{48,64},{64,80},{80,96},{96,112},{112,128},... | collective-permute-start | bytes 98312 | tf_op jit(solution)/shard_map/ppermute | solution.py:28
  67.5 0.5 copy.116
  68.0 0.6 copy.374
  68.6 0.6 copy.372
  69.2 1.9 %collective-permute-start.10 = (f32[2,24,256]{2,1,0:T(8,128)}, f32[2,24,256]{2,1,0:T(8,128)}, u32[]{:S(2)}, u32[]{:S(2)}) collective-permute-start(f32[2,24,256]{2,1,0:T(8,128)} %bitcast.128), channel_id=1, source_target_pairs={{1,0},{2,1},{3,2},{4,3},{5,4},{6,5},{7,6},{8,7},{9,8},{10,9},{11,1... | collective-permute-start | bytes 147464 | tf_op jit(solution)/shard_map/ppermute | solution.py:28
  71.2 2.4 %collective-permute-start.11 = (f32[2,24,256]{2,1,0:T(8,128)}, f32[2,24,256]{2,1,0:T(8,128)}, u32[]{:S(2)}, u32[]{:S(2)}) collective-permute-start(f32[2,24,256]{2,1,0:T(8,128)} %bitcast.130), channel_id=1, source_target_pairs={{0,1},{1,2},{2,3},{3,4},{4,5},{5,6},{6,7},{7,8},{8,9},{9,10},{10,1... | collective-permute-start | bytes 147464 | tf_op jit(solution)/shard_map/ppermute | solution.py:28
  73.6 0.6 copy_add_fusion.7
  74.2 0.9 scatter-add.26
  75.1 1.4 %slice_add_fusion.5 = f32[2,1,16,256]{3,1,0,2:T(1,128)} fusion(f32[2,24,16,256]{3,1,0,2:T(8,128)S(1)} %scatter-add.26, f32[2,16,256]{2,0,1:T(2,128)} %collective-permute-done.9), kind=kLoop, calls=%fused_computation.202 | loop fusion | flops 8192 | bytes 98304 | tf_op jit(solution)/shard_map/add | solution.py:100
  76.5 1.1 scatter-add.29
  77.6 0.8 fusion.55
  78.4 0.5 collective-permute-done.11
  79.0 0.8 fusion.54
  79.8 1.8 %multiply_negate_fusion = (f32[24,16,256]{2,0,1:T(8,128)S(1)}, f32[24,16,256]{2,0,1:T(8,128)S(1)}, f32[1,24,16,256]{3,1,2,0:T(8,128)S(1)}, f32[24,16,256]{2,0,1:T(8,128)S(1)}) fusion(f32[24,16,256]{2,1,0:T(8,128)S(1)} %copy-done, f32[24,16,256]{2,0,1:T(8,128)S(1)} %get-tuple-element.113, f32[2,24,16,256]{3,1,2,0:T(8,128)} %copy-done.3, ...), kind=kLoop, calls=%fused_computation.126 | loop fusion | flops 3047424 | bytes 3932160 | tf_op jit(solution)/shard_map/transpose(jvp())/neg | solution.py:52
  81.8 1.0 multiply_bitcast_fusion
  82.7 0.1 copy.129
  82.9 0.5 fusion.5
  83.4 0.5 multiply_add_fusion
  84.0 0.7 fusion.61
  84.7 1.3 %fusion.14 = (f32[24,16,256]{2,0,1:T(8,128)S(1)}, f32[1,24,16,256]{3,1,2,0:T(8,128)S(1)}) fusion(f32[24,16,256]{2,1,0:T(8,128)S(1)} %get-tuple-element.104, f32[24,16,256]{2,1,0:T(8,128)S(1)} %get-tuple-element.105, f32[24,16,256]{2,0,1:T(8,128)S(1)} %get-tuple-element.108, f32[24,16,256]{2,1,0:T(8,128)S(1)} %get-tuple-element.106, ...), kind=kLoop, calls=%fused_computation.72 | loop fusion | flops 4423680 | bytes 4718592 | tf_op jit(solution)/shard_map/transpose(jvp())/add_any | solution.py:51
  86.0 0.2 fusion.33
  86.2 0.1 copy.130
  86.4 0.5 pad_add_fusion
  86.9 6.9 %collective-permute-start.12 = (f32[2,16,256]{2,0,1:T(2,128)S(1)}, f32[2,16,256]{2,0,1:T(2,128)S(1)}, u32[]{:S(2)}, u32[]{:S(2)}) collective-permute-start(f32[2,16,256]{2,0,1:T(2,128)S(1)} %bitcast.145), channel_id=1, source_target_pairs={{16,0},{32,16},{48,32},{64,48},{80,64},{96,80},{112,96},{128,112},... | collective-permute-start | bytes 98312 | tf_op jit(solution)/shard_map/ppermute | solution.py:28
  94.0 1.9 %collective-permute-start.13 = (f32[2,16,256]{2,0,1:T(2,128)S(1)}, f32[2,16,256]{2,0,1:T(2,128)S(1)}, u32[]{:S(2)}, u32[]{:S(2)}) collective-permute-start(f32[2,16,256]{2,0,1:T(2,128)S(1)} %bitcast.146), channel_id=1, source_target_pairs={{0,16},{16,32},{32,48},{48,64},{64,80},{80,96},{96,112},{112,128},... | collective-permute-start | bytes 98312 | tf_op jit(solution)/shard_map/ppermute | solution.py:28
  96.0 0.5 copy.122
  96.5 4.5 %collective-permute-start.14 = (f32[2,24,256]{2,1,0:T(8,128)S(1)}, f32[2,24,256]{2,1,0:T(8,128)S(1)}, u32[]{:S(2)}, u32[]{:S(2)}) collective-permute-start(f32[2,24,256]{2,1,0:T(8,128)S(1)} %bitcast.144), channel_id=1, source_target_pairs={{1,0},{2,1},{3,2},{4,3},{5,4},{6,5},{7,6},{8,7},{9,8},{10,9},{11,1... | collective-permute-start | bytes 147464 | tf_op jit(solution)/shard_map/ppermute | solution.py:28
  100.9 1.9 %collective-permute-start.15 = (f32[2,24,256]{2,1,0:T(8,128)S(1)}, f32[2,24,256]{2,1,0:T(8,128)S(1)}, u32[]{:S(2)}, u32[]{:S(2)}) collective-permute-start(f32[2,24,256]{2,1,0:T(8,128)S(1)} %bitcast.143), channel_id=1, source_target_pairs={{0,1},{1,2},{2,3},{3,4},{4,5},{5,6},{6,7},{7,8},{8,9},{9,10},{10,1... | collective-permute-start | bytes 147464 | tf_op jit(solution)/shard_map/ppermute | solution.py:28
  102.9 0.1 scatter-add.34
  103.1 0.1 scatter-add.35
  103.3 5.1 %collective-permute-done.15 = f32[2,24,256]{2,1,0:T(8,128)S(1)} collective-permute-done((f32[2,24,256]{2,1,0:T(8,128)S(1)}, f32[2,24,256]{2,1,0:T(8,128)S(1)}, u32[]{:S(2)}, u32[]{:S(2)}) %collective-permute-start.15) | collective-permute-done | bytes 49184 | tf_op jit(solution)/shard_map/ppermute | solution.py:28
  108.5 0.9 copy.112
  109.4 0.9 copy.111
  (58 shorter events, 1.4 us)
Async XLA Ops:
  0.6 11.0 %copy-start.8 = (f32[16]{0:T(128)S(1)}, f32[16]{0:T(128)}, u32[]{:S(2)}) copy-start(f32[16]{0:T(128)} %param.32) | copy-start | bytes 196
  0.6 11.0 %copy-start.6 = (s32[24,16,256]{2,1,0:T(8,128)S(1)}, s32[24,16,256]{2,1,0:T(8,128)}, u32[]{:S(2)}) copy-start(s32[24,16,256]{2,1,0:T(8,128)} %param.30) | copy-start | bytes 1179652
  0.7 11.7 %copy-start.9 = (f32[8]{0:T(128)S(1)}, f32[8]{0:T(128)}, u32[]{:S(2)}) copy-start(f32[8]{0:T(128)} %param.33) | copy-start | bytes 100
  0.7 11.7 %copy-start.7 = (s32[24,16,256]{2,1,0:T(8,128)S(1)}, s32[24,16,256]{2,1,0:T(8,128)}, u32[]{:S(2)}) copy-start(s32[24,16,256]{2,1,0:T(8,128)} %param.29) | copy-start | bytes 1179652
  2.4 10.4 %collective-permute-start.1 = (f32[2,1,16,256]{3,1,2,0:T(1,128)S(1)}, f32[2,1,16,256]{3,1,2,0:T(1,128)S(1)}, u32[]{:S(2)}, u32[]{:S(2)}) collective-permute-start(f32[2,1,16,256]{3,1,2,0:T(1,128)S(1)} %get-tuple-element.145), channel_id=1, source_target_pairs={{0,16},{16,32},{32,48},{48,64},{64,80},{80,96},{96,112},{112,128},... | collective-permute-start | bytes 98312 | tf_op jit(solution)/shard_map/ppermute | solution.py:19
  7.6 7.4 %collective-permute-start = (f32[2,1,16,256]{3,1,2,0:T(1,128)S(1)}, f32[2,1,16,256]{3,1,2,0:T(1,128)S(1)}, u32[]{:S(2)}, u32[]{:S(2)}) collective-permute-start(f32[2,1,16,256]{3,1,2,0:T(1,128)S(1)} %get-tuple-element.146), channel_id=1, source_target_pairs={{16,0},{32,16},{48,32},{64,48},{80,64},{96,80},{112,96},{128,112},... | collective-permute-start | bytes 98312 | tf_op jit(solution)/shard_map/ppermute | solution.py:20
  15.0 5.7 %collective-permute-start.2 = (f32[2,26,1,256]{3,1,2,0:T(8,128)S(1)}, f32[2,26,1,256]{3,1,2,0:T(8,128)S(1)}, u32[]{:S(2)}, u32[]{:S(2)}) collective-permute-start(f32[2,26,1,256]{3,1,2,0:T(8,128)S(1)} %get-tuple-element.138), channel_id=1, source_target_pairs={{1,0},{2,1},{3,2},{4,3},{5,4},{6,5},{7,6},{8,7},{9,8},{10,9},{11,1... | collective-permute-start | bytes 159752 | tf_op jit(solution)/shard_map/ppermute | solution.py:20
  18.6 7.7 %collective-permute-start.3 = (f32[2,26,1,256]{3,1,2,0:T(8,128)S(1)}, f32[2,26,1,256]{3,1,2,0:T(8,128)S(1)}, u32[]{:S(2)}, u32[]{:S(2)}) collective-permute-start(f32[2,26,1,256]{3,1,2,0:T(8,128)S(1)} %get-tuple-element.139), channel_id=1, source_target_pairs={{0,1},{1,2},{2,3},{3,4},{4,5},{5,6},{6,7},{7,8},{8,9},{9,10},{10,1... | collective-permute-start | bytes 159752 | tf_op jit(solution)/shard_map/ppermute | solution.py:19
  20.6 6.3 %copy-start = (f32[24,16,256]{2,1,0:T(8,128)S(1)}, f32[24,16,256]{2,1,0:T(8,128)}, u32[]{:S(2)}) copy-start(f32[24,16,256]{2,1,0:T(8,128)} %param.25) | copy-start | bytes 1179652
  20.6 6.3 %copy-start.1 = (s32[24,16,256]{2,1,0:T(8,128)S(1)}, s32[24,16,256]{2,1,0:T(8,128)}, u32[]{:S(2)}) copy-start(s32[24,16,256]{2,1,0:T(8,128)} %param.31) | copy-start | bytes 1179652
  20.6 6.3 %copy-start.2 = (f32[24,16,256]{2,1,0:T(8,128)S(1)}, f32[24,16,256]{2,1,0:T(8,128)}, u32[]{:S(2)}) copy-start(f32[24,16,256]{2,1,0:T(8,128)} %param.26) | copy-start | bytes 1179652
  27.0 1.2 %copy-start.3 = (f32[2,24,16,256]{3,1,2,0:T(8,128)}, f32[2,24,16,256]{3,1,2,0:T(8,128)S(1)}, u32[]{:S(2)}) copy-start(f32[2,24,16,256]{3,1,2,0:T(8,128)S(1)} %fusion.2) | copy-start | bytes 2359300
  29.2 8.9 %collective-permute-start.5 = (f32[2,1,16,256]{3,1,2,0:T(1,128)S(1)}, f32[2,1,16,256]{3,1,2,0:T(1,128)S(1)}, u32[]{:S(2)}, u32[]{:S(2)}) collective-permute-start(f32[2,1,16,256]{3,1,2,0:T(1,128)S(1)} %get-tuple-element.143), channel_id=1, source_target_pairs={{0,16},{16,32},{32,48},{48,64},{64,80},{80,96},{96,112},{112,128},... | collective-permute-start | bytes 98312 | tf_op jit(solution)/shard_map/ppermute | solution.py:19
  35.0 6.7 %collective-permute-start.4 = (f32[2,1,16,256]{3,1,2,0:T(1,128)S(1)}, f32[2,1,16,256]{3,1,2,0:T(1,128)S(1)}, u32[]{:S(2)}, u32[]{:S(2)}) collective-permute-start(f32[2,1,16,256]{3,1,2,0:T(1,128)S(1)} %get-tuple-element.144), channel_id=1, source_target_pairs={{16,0},{32,16},{48,32},{64,48},{80,64},{96,80},{112,96},{128,112},... | collective-permute-start | bytes 98312 | tf_op jit(solution)/shard_map/ppermute | solution.py:20
  41.7 4.6 %collective-permute-start.6 = (f32[2,26,1,256]{3,1,2,0:T(8,128)S(1)}, f32[2,26,1,256]{3,1,2,0:T(8,128)S(1)}, u32[]{:S(2)}, u32[]{:S(2)}) collective-permute-start(f32[2,26,1,256]{3,1,2,0:T(8,128)S(1)} %get-tuple-element.136), channel_id=1, source_target_pairs={{1,0},{2,1},{3,2},{4,3},{5,4},{6,5},{7,6},{8,7},{9,8},{10,9},{11,1... | collective-permute-start | bytes 159752 | tf_op jit(solution)/shard_map/ppermute | solution.py:20
  43.7 7.7 %collective-permute-start.7 = (f32[2,26,1,256]{3,1,2,0:T(8,128)S(1)}, f32[2,26,1,256]{3,1,2,0:T(8,128)S(1)}, u32[]{:S(2)}, u32[]{:S(2)}) collective-permute-start(f32[2,26,1,256]{3,1,2,0:T(8,128)S(1)} %get-tuple-element.137), channel_id=1, source_target_pairs={{0,1},{1,2},{2,3},{3,4},{4,5},{5,6},{6,7},{7,8},{8,9},{9,10},{10,1... | collective-permute-start | bytes 159752 | tf_op jit(solution)/shard_map/ppermute | solution.py:19
  51.9 1.0 copy-start.4
  51.9 1.1 %copy-start.5 = (f32[24,16,256]{2,1,0:T(8,128)S(1)}, f32[24,16,256]{2,1,0:T(8,128)}, u32[]{:S(2)}) copy-start(f32[24,16,256]{2,1,0:T(8,128)} %param.28) | copy-start | bytes 1179652
  59.6 14.0 %collective-permute-start.8 = (f32[2,16,256]{2,0,1:T(2,128)S(1)}, f32[2,16,256]{2,0,1:T(2,128)S(1)}, u32[]{:S(2)}, u32[]{:S(2)}) collective-permute-start(f32[2,16,256]{2,0,1:T(2,128)S(1)} %bitcast.147), channel_id=1, source_target_pairs={{16,0},{32,16},{48,32},{64,48},{80,64},{96,80},{112,96},{128,112},... | collective-permute-start | bytes 98312 | tf_op jit(solution)/shard_map/ppermute | solution.py:28
  65.6 9.5 %collective-permute-start.9 = (f32[2,16,256]{2,0,1:T(2,128)}, f32[2,16,256]{2,0,1:T(2,128)}, u32[]{:S(2)}, u32[]{:S(2)}) collective-permute-start(f32[2,16,256]{2,0,1:T(2,128)} %bitcast.133), channel_id=1, source_target_pairs={{0,16},{16,32},{32,48},{48,64},{64,80},{80,96},{96,112},{112,128},... | collective-permute-start | bytes 98312 | tf_op jit(solution)/shard_map/ppermute | solution.py:28
  69.2 8.4 %collective-permute-start.10 = (f32[2,24,256]{2,1,0:T(8,128)}, f32[2,24,256]{2,1,0:T(8,128)}, u32[]{:S(2)}, u32[]{:S(2)}) collective-permute-start(f32[2,24,256]{2,1,0:T(8,128)} %bitcast.128), channel_id=1, source_target_pairs={{1,0},{2,1},{3,2},{4,3},{5,4},{6,5},{7,6},{8,7},{9,8},{10,9},{11,1... | collective-permute-start | bytes 147464 | tf_op jit(solution)/shard_map/ppermute | solution.py:28
  71.2 7.8 %collective-permute-start.11 = (f32[2,24,256]{2,1,0:T(8,128)}, f32[2,24,256]{2,1,0:T(8,128)}, u32[]{:S(2)}, u32[]{:S(2)}) collective-permute-start(f32[2,24,256]{2,1,0:T(8,128)} %bitcast.130), channel_id=1, source_target_pairs={{0,1},{1,2},{2,3},{3,4},{4,5},{5,6},{6,7},{7,8},{8,9},{9,10},{10,1... | collective-permute-start | bytes 147464 | tf_op jit(solution)/shard_map/ppermute | solution.py:28
  86.9 16.0 %collective-permute-start.12 = (f32[2,16,256]{2,0,1:T(2,128)S(1)}, f32[2,16,256]{2,0,1:T(2,128)S(1)}, u32[]{:S(2)}, u32[]{:S(2)}) collective-permute-start(f32[2,16,256]{2,0,1:T(2,128)S(1)} %bitcast.145), channel_id=1, source_target_pairs={{16,0},{32,16},{48,32},{64,48},{80,64},{96,80},{112,96},{128,112},... | collective-permute-start | bytes 98312 | tf_op jit(solution)/shard_map/ppermute | solution.py:28
  94.0 9.1 %collective-permute-start.13 = (f32[2,16,256]{2,0,1:T(2,128)S(1)}, f32[2,16,256]{2,0,1:T(2,128)S(1)}, u32[]{:S(2)}, u32[]{:S(2)}) collective-permute-start(f32[2,16,256]{2,0,1:T(2,128)S(1)} %bitcast.146), channel_id=1, source_target_pairs={{0,16},{16,32},{32,48},{48,64},{64,80},{80,96},{96,112},{112,128},... | collective-permute-start | bytes 98312 | tf_op jit(solution)/shard_map/ppermute | solution.py:28
  96.5 6.8 %collective-permute-start.14 = (f32[2,24,256]{2,1,0:T(8,128)S(1)}, f32[2,24,256]{2,1,0:T(8,128)S(1)}, u32[]{:S(2)}, u32[]{:S(2)}) collective-permute-start(f32[2,24,256]{2,1,0:T(8,128)S(1)} %bitcast.144), channel_id=1, source_target_pairs={{1,0},{2,1},{3,2},{4,3},{5,4},{6,5},{7,6},{8,7},{9,8},{10,9},{11,1... | collective-permute-start | bytes 147464 | tf_op jit(solution)/shard_map/ppermute | solution.py:28
  100.9 7.5 %collective-permute-start.15 = (f32[2,24,256]{2,1,0:T(8,128)S(1)}, f32[2,24,256]{2,1,0:T(8,128)S(1)}, u32[]{:S(2)}, u32[]{:S(2)}) collective-permute-start(f32[2,24,256]{2,1,0:T(8,128)S(1)} %bitcast.143), channel_id=1, source_target_pairs={{0,1},{1,2},{2,3},{3,4},{4,5},{5,6},{6,7},{7,8},{8,9},{9,10},{10,1... | collective-permute-start | bytes 147464 | tf_op jit(solution)/shard_map/ppermute | solution.py:28
where the time goes:
time: 111 us; the launch traced here: 110 us
  starting transfers between devices  54.8 us (49%)
  waiting for transfers between devices  22.2 us (20%)
  other arithmetic  21.9 us (20%)
  local copies, waits for them, and re-layouts  10 us (9%)
  between operations  1.36 us (1%)
    ppermute x8, starting transfers between devices, passed_along(): return lax.ppermute(shard, axis, pairs)  26.7 us
    ppermute x4, starting transfers between devices, extended(): before = lax.ppermute(last, axis, up)  15.4 us
    ppermute x4, starting transfers between devices, extended(): after = lax.ppermute(leading, axis, down)  12.7 us
    ppermute x4, waiting for transfers between devices, extended(): before = lax.ppermute(last, axis, up)  10.7 us
    ppermute x4, waiting for transfers between devices, extended(): after = lax.ppermute(leading, axis, down)  5.78 us
    unnamed x36, local copies, waits for them, and re-layouts  5.74 us
    ppermute x8, waiting for transfers between devices, passed_along(): return lax.ppermute(shard, axis, pairs)  5.7 us
    add_any x2, other arithmetic, reaction(): denominator = phase * phase + (1.0 - phase) * (1.0 - phase)  3.2 us
  transfers between devices with their start and end apart: 16, of which 6 were waited for; matrix products, arithmetic and copies ran while one was open for 9% of the time, Pallas kernels for 0%

commit v1 on v0

v1 whole, which is shorter than its diff:
```python
import functools

import jax
import jax.numpy as jnp
from jax import lax
from jax.experimental import pallas as pl
from jax.experimental.pallas import tpu as pltpu
from jax.sharding import PartitionSpec as P

mobility_step = 0.1
well_height = 1.0
coupling = 1.0
diffusion_step = 0.03

MESH = pl.DeviceIdType.MESH


def pick(index, table, count):
    values = [table[k] for k in range(count)]
    bit = 1
    while len(values) > 1:
        odd = (index & bit) != 0
        values = [jnp.where(odd, values[k + 1], values[k]) for k in range(0, len(values), 2)]
        bit *= 2
    return values[0]


def local_terms(phase, jump):
    t = phase - phase * phase
    inverse = 1.0 / (1.0 - 2.0 * t)
    slope = 2.0 * t * inverse * inverse
    slope_derivative = 2.0 * (1.0 - 2.0 * phase) * (1.0 + 2.0 * t) * (inverse * inverse * inverse)
    release = 1.0 / (1.0 - jump * (phase * phase * inverse))
    return t, slope, slope_derivative, release


def kernel(
    nx_dev, ny_dev,
    p_hbm, m_hbm, a_hbm, b_hbm, or_hbm, an_hbm, bm_hbm, st, pt,
    out_p, out_m,
    P0, M0, A, B, OR, AN, BM, P1, M1, U1, V1, U0, V0,
    KAP, JMP, MOV, JS0, W0, G0, K0,
    load_sem, ss, rs,
):
    X, Y, Z = p_hbm.shape
    HI, LO = Y, Y + 7
    gx, gy = lax.axis_index("gx"), lax.axis_index("gy")
    has = {
        ("x", 0): gx > 0, ("x", 1): gx < nx_dev - 1,
        ("y", 0): gy > 0, ("y", 1): gy < ny_dev - 1,
    }
    device = {
        ("x", 0): {"gx": gx - 1}, ("x", 1): {"gx": gx + 1},
        ("y", 0): {"gy": gy - 1}, ("y", 1): {"gy": gy + 1},
    }

    loads = []
    for k, (src, dst, off) in enumerate((
        (p_hbm, P0, 2), (m_hbm, M0, 2), (or_hbm, OR, 1), (an_hbm, AN, 1),
        (bm_hbm, BM, 1), (a_hbm, A, 1), (b_hbm, B, 1),
    )):
        copy = pltpu.make_async_copy(src, dst.at[pl.ds(off, X), pl.ds(0, Y), :], load_sem.at[k])
        copy.start()
        loads.append(copy)

    barrier = pltpu.get_barrier_semaphore()
    count = jnp.int32(0)
    for key, there in has.items():
        @pl.when(there)
        def _():
            pl.semaphore_signal(barrier, inc=1, device_id=device[key], device_id_type=MESH)
        count = count + there.astype(jnp.int32)

    for side, (two, one) in enumerate(((0, 0), (X + 2, X + 1))):
        @pl.when(jnp.logical_not(has["x", side]))
        def _():
            for ref in (P0, M0):
                ref[pl.ds(two, 2)] = jnp.zeros((2,) + ref.shape[1:], ref.dtype)
            for ref in (A, B, OR, AN):
                ref[one] = jnp.zeros(ref.shape[1:], ref.dtype)
            BM[one] = jnp.ones(BM.shape[1:], BM.dtype)
            for ref in (U0, V0):
                ref[one] = jnp.zeros(ref.shape[1:], ref.dtype)
    for side, row in enumerate((LO, HI)):
        @pl.when(jnp.logical_not(has["y", side]))
        def _():
            for ref, off in ((P0, 2), (M0, 2), (P1, 1), (M1, 1), (U1, 1), (V1, 1), (U0, 1), (V0, 1)):
                ref[pl.ds(off, X), pl.ds(row, 1), :] = jnp.zeros((X, 1, Z), ref.dtype)

    sems = iter(range(ss.shape[0]))

    def exchange(axis, pieces):
        sends = {0: [], 1: []}
        arrivals = {0: [], 1: []}
        for ref, down, down_to, up, up_to in pieces:
            for side, src, dst in ((0, down, down_to), (1, up, up_to)):
                k = next(sems)
                copy = pltpu.make_async_remote_copy(
                    src_ref=ref.at[src], dst_ref=ref.at[dst], send_sem=ss.at[k], recv_sem=rs.at[k],
                    device_id=device[axis, side], device_id_type=MESH,
                )
                sends[side].append(copy)
                arrivals[1 - side].append(copy)

        def start():
            for side in (0, 1):
                @pl.when(has[axis, side])
                def _():
                    for copy in sends[side]:
                        copy.start()

        def wait_recv():
            for side in (0, 1):
                @pl.when(has[axis, side])
                def _():
                    for copy in arrivals[side]:
                        copy.wait_recv()

        def wait_send():
            for side in (0, 1):
                @pl.when(has[axis, side])
                def _():
                    for copy in sends[side]:
                        copy.wait_send()

        return start, wait_recv, wait_send

    rows = pl.ds(0, Y)

    def x_layers(ref, off, width):
        return (
            ref,
            (pl.ds(off, width), rows), (pl.ds(off + X, width), rows),
            (pl.ds(off + X - width, width), rows), (pl.ds(off - width, width), rows),
        )

    def y_rows(ref, off):
        own = pl.ds(off, X)
        return ref, (own, 0), (own, HI), (own, Y - 1), (own, LO)

    def corner(ref):
        tile = pl.ds(Y, 8)
        return ref, (2, tile), (X + 2, tile), (X + 1, tile), (1, tile)

    x_state = exchange("x", [x_layers(ref, 2, 2) for ref in (P0, M0)])
    y_state = exchange("y", [y_rows(ref, 2) for ref in (P0, M0)])
    x_rest = exchange("x", [x_layers(ref, 1, 1) for ref in (OR, AN, BM, A, B)])
    x_corner = exchange("x", [corner(ref) for ref in (P0, M0)])
    y_middle = exchange("y", [y_rows(ref, 1) for ref in (P1, M1, U1, V1)])
    x_last = exchange("x", [x_layers(ref, 1, 1) for ref in (U0, V0)])
    y_last = exchange("y", [y_rows(ref, 1) for ref in (U0, V0)])

    loads[0].wait()
    loads[1].wait()
    pl.semaphore_wait(barrier, count)
    x_state[0]()
    y_state[0]()
    for copy in loads[2:]:
        copy.wait()
    x_rest[0]()

    lane = lax.broadcasted_iota(jnp.int32, (Y, Z), 1)
    first, last = lane == 0, lane == Z - 1

    def lap(ref, i):
        wide = ref[i]
        center = wide[:Y]
        beside = ref[i - 1, :Y] + ref[i + 1, :Y]
        beside = beside + pltpu.roll(wide, Y + 7, 0)[:Y] + pltpu.roll(wide, 1, 0)[:Y]
        beside = beside + jnp.where(first, 0.0, pltpu.roll(center, 1, 1))
        beside = beside + jnp.where(last, 0.0, pltpu.roll(center, Z - 1, 1))
        return beside - 6.0 * center

    def tables(x):
        i = x + 1
        KAP[i] = pick(AN[i], st, st.shape[0])
        JMP[i] = 1.0 - pick(OR[i], pt, pt.shape[0])
        MOV[i] = 1.0 - BM[i].astype(jnp.float32)

    def forward(x, own):
        i = x + 1
        phase, potential = P0[x + 2, :Y], M0[x + 2, :Y]
        lap_phase, lap_potential = lap(P0, x + 2), lap(M0, x + 2)
        stiffness, jump, movable = KAP[i], JMP[i], MOV[i]
        t, slope, slope_derivative, release = local_terms(phase, jump)
        held_slope = jump * slope
        drive = (
            stiffness * lap_phase
            - 2.0 * well_height * t * (1.0 - 2.0 * phase)
            + coupling * held_slope * potential
        )
        step = movable * mobility_step * drive
        flux = (diffusion_step * lap_potential - held_slope * step) * release
        phase_next = phase + step
        potential_next = potential + movable * flux
        P1[i, :Y] = phase_next
        M1[i, :Y] = potential_next
        if own:
            JS0[x] = held_slope
            W0[x] = movable * release
            G0[x] = well_height * (12.0 * t - 2.0) + coupling * jump * slope_derivative * potential
            K0[x] = jump * (slope * flux - step * slope_derivative)
        _, slope, _, release = local_terms(phase_next, jump)
        spread = B[i] * (movable * release)
        pull = mobility_step * movable * (A[i] - spread * (jump * slope))
        U1[i, :Y] = stiffness * pull
        V1[i, :Y] = diffusion_step * spread

    def backward(x):
        i = x + 1
        phase, potential = P1[i, :Y], M1[i, :Y]
        stiffness, jump, movable = KAP[i], JMP[i], MOV[i]
        t, slope, slope_derivative, release = local_terms(phase, jump)
        held_slope = jump * slope
        drive = (
            stiffness * lap(P1, i)
            - 2.0 * well_height * t * (1.0 - 2.0 * phase)
            + coupling * held_slope * potential
        )
        step = movable * mobility_step * drive
        flux = (diffusion_step * lap(M1, i) - held_slope * step) * release
        gain = well_height * (12.0 * t - 2.0) + coupling * jump * slope_derivative * potential
        keep = jump * (slope * flux - step * slope_derivative)
        spread = B[i] * (movable * release)
        pull = mobility_step * movable * (A[i] - spread * held_slope)
        bar_p = A[i] + pull * gain + spread * keep + lap(U1, i)
        bar_m = B[i] + coupling * held_slope * pull + lap(V1, i)
        spread = bar_m * W0[x]
        pull = mobility_step * movable * (bar_p - spread * JS0[x])
        U0[i, :Y] = stiffness * pull
        V0[i, :Y] = diffusion_step * spread
        out_p[x] = bar_p + pull * G0[x] + spread * K0[x]
        out_m[x] = bar_m + coupling * JS0[x] * pull

    def finish(x):
        out_p[x] = out_p[x] + lap(U0, x + 1)
        out_m[x] = out_m[x] + lap(V0, x + 1)

    def over(low, high, body):
        def step(x, carry):
            body(x)
            return carry
        lax.fori_loop(low, high, step, 0)

    over(0, X, tables)
    y_state[1]()
    x_corner[0]()
    over(1, X - 1, lambda x: forward(x, True))
    x_state[1]()
    over(0, 2, lambda k: forward(k * (X - 1), True))
    y_middle[0]()
    x_rest[1]()
    x_corner[1]()
    over(0, 2, lambda k: tables(k * (X + 1) - 1))
    over(0, 2, lambda k: forward(k * (X + 1) - 1, False))
    y_middle[1]()
    over(0, 2, lambda k: backward(k * (X - 1)))
    x_last[0]()
    over(1, X - 1, backward)
    y_last[0]()
    y_last[1]()
    over(1, X - 1, finish)
    x_last[1]()
    over(0, 2, lambda k: finish(k * (X - 1)))
    for step in (x_state, y_state, x_rest, x_corner, y_middle, x_last, y_last):
        step[2]()


def hand_over(p_ref, m_ref, p_out, m_out, sem):
    copies = [pltpu.make_async_copy(p_ref, p_out, sem.at[0]), pltpu.make_async_copy(m_ref, m_out, sem.at[1])]
    for copy in copies:
        copy.start()
    for copy in copies:
        copy.wait()


def solution(mesh):
    nx_dev, ny_dev = mesh.shape["gx"], mesh.shape["gy"]
    split = P("gx", "gy", None)

    def on_device(*args):
        X, Y, Z = args[0].shape
        f32, i32 = jnp.float32, jnp.int32
        anywhere = pl.BlockSpec(memory_space=pl.ANY)
        scalars = pl.BlockSpec(memory_space=pltpu.SMEM)
        vmem = pltpu.VMEM
        copies = 2 * (2 + 2 + 5 + 2 + 4 + 2 + 2)
        results = pl.pallas_call(
            functools.partial(kernel, nx_dev, ny_dev),
            out_shape=[vmem((X, Y, Z), f32)] * 2,
            in_specs=[anywhere] * 7 + [scalars] * 2,
            out_specs=[pl.BlockSpec(memory_space=vmem)] * 2,
            scratch_shapes=(
                [vmem((X + 4, Y + 8, Z), f32)] * 2
                + [vmem((X + 2, Y, Z), f32)] * 2
                + [vmem((X + 2, Y, Z), i32)] * 3
                + [vmem((X + 2, Y + 8, Z), f32)] * 6
                + [vmem((X + 2, Y, Z), f32)] * 3
                + [vmem((X, Y, Z), f32)] * 4
                + [pltpu.SemaphoreType.DMA((7,))]
                + [pltpu.SemaphoreType.DMA((copies,))] * 2
            ),
            compiler_params=pltpu.CompilerParams(
                collective_id=0, has_side_effects=True, vmem_limit_bytes=32 * 1024 * 1024
            ),
            name="reverse",
        )(*args)
        return pl.pallas_call(
            hand_over,
            out_shape=[jax.ShapeDtypeStruct((X, Y, Z), f32)] * 2,
            in_specs=[pl.BlockSpec(memory_space=vmem)] * 2,
            out_specs=[anywhere] * 2,
            scratch_shapes=[pltpu.SemaphoreType.DMA((2,))],
            name="hand_over",
        )(*results)

    return jax.shard_map(
        on_device, mesh=mesh, in_specs=(split,) * 7 + (P(), P()), out_specs=(split, split), check_vma=False
    )
```

time: 111 us -> 44.9 us (0.40)
  starting transfers between devices: 54.8 us -> 0 us
  Pallas kernels: 0 us -> 34.1 us
  waiting for transfers between devices: 22.2 us -> 0 us
  other arithmetic: 21.9 us -> 0 us
    ppermute x16 -> x0, starting transfers between devices: 54.8 us -> none  [the longest x8 26.7 us: passed_along(): return lax.ppermute(shard, axis, pairs)]
    pallas_call x0 -> x2, Pallas kernels: none -> 34.1 us  [the longest x1 32.1 us: on_device(): pl.pallas_call(functools.partial(kernel, nx_dev, ny_dev), out_shape=[vmem...]
    ppermute x16 -> x0, waiting for transfers between devices: 22.2 us -> none  [the longest x4 10.7 us: extended(): before = lax.ppermute(last, axis, up)]
    add_any x12 -> x0, other arithmetic: 7.64 us -> none  [the longest x2 3.2 us: reaction(): denominator = phase * phase + (1.0 - phase) * (1.0 - phase)]
    unnamed x36 -> x22, local copies, waits for them, and re-layouts: 5.74 us -> 9.75 us
    add x6 -> x0, other arithmetic: 3.61 us -> none  [the longest x2 1.42 us: on_device(): interior = interior.at[:, 0, :, :].add(from_below)]
    scatter-add x4 -> x0, local copies, waits for them, and re-layouts: 2.28 us -> none  [the longest x2 1.25 us: on_device(): interior = interior.at[:, 0, :, :].add(from_below)]
    mul x3 -> x0, other arithmetic: 2.18 us -> none  [the longest x2 1.64 us: reaction(): denominator = phase * phase + (1.0 - phase) * (1.0 - phase)]
  transfers between devices with their start and end apart: 16 -> 0, of which waited for: 6 -> 0; matrix products, arithmetic and copies ran while one was open for 9% -> 0% of each run, Pallas kernels for 0% -> 0%
where the time goes in v1:
time: 44.9 us; the launch traced here: 44.5 us
  Pallas kernels  34.1 us (76%)
  local copies, waits for them, and re-layouts  9.75 us (22%)
  between operations  0.67 us (1%)
    pallas_call x1, Pallas kernels, on_device(): pl.pallas_call(functools.partial(kernel, nx_dev, ny_dev), out_shape=[vmem...  32.1 us
    unnamed x22, local copies, waits for them, and re-layouts  9.75 us
    pallas_call x1, Pallas kernels, on_device(): pl.pallas_call(hand_over, out_shape=[jax.ShapeDtypeStruct((X, Y, Z), f32)...  2 us

profile of v1, /device:TPU:34, one launch (start us, length us, event | category | flops | bytes accessed | tf_op | source)
XLA Modules:
  0.0 44.5 jit_solution(12572903762475309312)
XLA Ops:
  0.6 0.0 copy-start
  0.6 1.0 %copy-done = f32[24,16,256]{2,1,0:T(8,128)S(1)} copy-done((f32[24,16,256]{2,1,0:T(8,128)S(1)}, f32[24,16,256]{2,1,0:T(8,128)}, u32[]{:S(2)}) %copy-start) | copy-done | bytes 393240
  1.6 0.0 copy-start.1
  1.6 1.0 %copy-done.1 = f32[24,16,256]{2,1,0:T(8,128)S(1)} copy-done((f32[24,16,256]{2,1,0:T(8,128)S(1)}, f32[24,16,256]{2,1,0:T(8,128)}, u32[]{:S(2)}) %copy-start.1) | copy-done | bytes 393240
  2.6 0.0 copy-start.2
  2.6 1.0 %copy-done.2 = f32[24,16,256]{2,1,0:T(8,128)S(1)} copy-done((f32[24,16,256]{2,1,0:T(8,128)S(1)}, f32[24,16,256]{2,1,0:T(8,128)}, u32[]{:S(2)}) %copy-start.2) | copy-done | bytes 393240
  3.6 0.0 copy-start.3
  3.6 1.0 %copy-done.3 = f32[24,16,256]{2,1,0:T(8,128)S(1)} copy-done((f32[24,16,256]{2,1,0:T(8,128)S(1)}, f32[24,16,256]{2,1,0:T(8,128)}, u32[]{:S(2)}) %copy-start.3) | copy-done | bytes 393240
  4.6 0.0 copy-start.4
  4.6 1.0 %copy-done.4 = s32[24,16,256]{2,1,0:T(8,128)S(1)} copy-done((s32[24,16,256]{2,1,0:T(8,128)S(1)}, s32[24,16,256]{2,1,0:T(8,128)}, u32[]{:S(2)}) %copy-start.4) | copy-done | bytes 393240
  5.6 0.0 copy-start.5
  5.6 1.0 %copy-done.5 = s32[24,16,256]{2,1,0:T(8,128)S(1)} copy-done((s32[24,16,256]{2,1,0:T(8,128)S(1)}, s32[24,16,256]{2,1,0:T(8,128)}, u32[]{:S(2)}) %copy-start.5) | copy-done | bytes 393240
  6.6 0.0 copy-start.6
  6.6 1.0 %copy-done.6 = s32[24,16,256]{2,1,0:T(8,128)S(1)} copy-done((s32[24,16,256]{2,1,0:T(8,128)S(1)}, s32[24,16,256]{2,1,0:T(8,128)}, u32[]{:S(2)}) %copy-start.6) | copy-done | bytes 393240
  7.6 0.0 copy-start.9
  7.6 0.7 %copy-done.9 = f32[16]{0:T(128)S(1)} copy-done((f32[16]{0:T(128)S(1)}, f32[16]{0:T(128)}, u32[]{:S(2)}) %copy-start.9) | copy-done | bytes 88
  8.3 0.0 copy-start.10
  8.3 0.7 %copy-done.10 = f32[8]{0:T(128)S(1)} copy-done((f32[8]{0:T(128)S(1)}, f32[8]{0:T(128)}, u32[]{:S(2)}) %copy-start.10) | copy-done | bytes 56
  8.9 32.1 %reverse.1 = (f32[24,16,256]{2,1,0:T(8,128)S(1)}, f32[24,16,256]{2,1,0:T(8,128)S(1)}) custom-call(f32[24,16,256]{2,1,0:T(8,128)S(1)} %copy-done, f32[24,16,256]{2,1,0:T(8,128)S(1)} %copy-done.1, f32[24,16,256]{2,1,0:T(8,128)S(1)} %copy-done.2, f32[24,16,256]{2,1,0:T(8,128)S(1)} %copy-done.3, s32[24,16,256]{2,1,0:T(8,128)S(1)} %copy-done.4, ...), custom_call_target="tpu_custom_call" | custom-call | tf_op jit(solution)/shard_map/reverse/pallas_call | solution.py:288
  41.0 0.0 copy-start.7
  41.1 0.7 %copy-done.7 = f32[24,16,256]{2,1,0:T(8,128)} copy-done((f32[24,16,256]{2,1,0:T(8,128)}, f32[24,16,256]{2,1,0:T(8,128)S(1)}, u32[]{:S(2)}) %copy-start.7) | copy-done | bytes 393240
  41.8 0.0 copy-start.8
  41.8 0.7 %copy-done.8 = f32[24,16,256]{2,1,0:T(8,128)} copy-done((f32[24,16,256]{2,1,0:T(8,128)}, f32[24,16,256]{2,1,0:T(8,128)S(1)}, u32[]{:S(2)}) %copy-start.8) | copy-done | bytes 393240
  42.5 2.0 %hand_over.1 = (f32[24,16,256]{2,1,0:T(8,128)}, f32[24,16,256]{2,1,0:T(8,128)}) custom-call(f32[24,16,256]{2,1,0:T(8,128)} %copy-done.7, f32[24,16,256]{2,1,0:T(8,128)} %copy-done.8), custom_call_target="tpu_custom_call" | custom-call | tf_op jit(solution)/shard_map/hand_over/pallas_call | solution.py:308
Async XLA Ops:
  0.6 1.0 %copy-start = (f32[24,16,256]{2,1,0:T(8,128)S(1)}, f32[24,16,256]{2,1,0:T(8,128)}, u32[]{:S(2)}) copy-start(f32[24,16,256]{2,1,0:T(8,128)} %p_hbm.1) | copy-start | bytes 1179652
  1.6 1.0 %copy-start.1 = (f32[24,16,256]{2,1,0:T(8,128)S(1)}, f32[24,16,256]{2,1,0:T(8,128)}, u32[]{:S(2)}) copy-start(f32[24,16,256]{2,1,0:T(8,128)} %m_hbm.1) | copy-start | bytes 1179652
  2.6 1.0 %copy-start.2 = (f32[24,16,256]{2,1,0:T(8,128)S(1)}, f32[24,16,256]{2,1,0:T(8,128)}, u32[]{:S(2)}) copy-start(f32[24,16,256]{2,1,0:T(8,128)} %a_hbm.1) | copy-start | bytes 1179652
  3.6 1.0 %copy-start.3 = (f32[24,16,256]{2,1,0:T(8,128)S(1)}, f32[24,16,256]{2,1,0:T(8,128)}, u32[]{:S(2)}) copy-start(f32[24,16,256]{2,1,0:T(8,128)} %b_hbm.1) | copy-start | bytes 1179652
  4.6 1.0 %copy-start.4 = (s32[24,16,256]{2,1,0:T(8,128)S(1)}, s32[24,16,256]{2,1,0:T(8,128)}, u32[]{:S(2)}) copy-start(s32[24,16,256]{2,1,0:T(8,128)} %or_hbm.1) | copy-start | bytes 1179652
  5.6 1.0 %copy-start.5 = (s32[24,16,256]{2,1,0:T(8,128)S(1)}, s32[24,16,256]{2,1,0:T(8,128)}, u32[]{:S(2)}) copy-start(s32[24,16,256]{2,1,0:T(8,128)} %an_hbm.1) | copy-start | bytes 1179652
  6.6 1.0 %copy-start.6 = (s32[24,16,256]{2,1,0:T(8,128)S(1)}, s32[24,16,256]{2,1,0:T(8,128)}, u32[]{:S(2)}) copy-start(s32[24,16,256]{2,1,0:T(8,128)} %bm_hbm.1) | copy-start | bytes 1179652
  7.6 0.7 %copy-start.9 = (f32[16]{0:T(128)S(1)}, f32[16]{0:T(128)}, u32[]{:S(2)}) copy-start(f32[16]{0:T(128)} %st.1) | copy-start | bytes 196
  8.3 0.7 %copy-start.10 = (f32[8]{0:T(128)S(1)}, f32[8]{0:T(128)}, u32[]{:S(2)}) copy-start(f32[8]{0:T(128)} %pt.1) | copy-start | bytes 100
  41.0 0.7 %copy-start.7 = (f32[24,16,256]{2,1,0:T(8,128)}, f32[24,16,256]{2,1,0:T(8,128)S(1)}, u32[]{:S(2)}) copy-start(f32[24,16,256]{2,1,0:T(8,128)S(1)} %get-tuple-element.4.p_ref) | copy-start | bytes 1179652
  41.8 0.7 %copy-start.8 = (f32[24,16,256]{2,1,0:T(8,128)}, f32[24,16,256]{2,1,0:T(8,128)S(1)}, u32[]{:S(2)}) copy-start(f32[24,16,256]{2,1,0:T(8,128)S(1)} %get-tuple-element.5.m_ref) | copy-start | bytes 1179652

commit v2 on v1

--- a/solution.py
+++ b/solution.py
@@ -36,10 +36,10 @@
 
 def kernel(
     nx_dev, ny_dev,
-    p_hbm, m_hbm, a_hbm, b_hbm, or_hbm, an_hbm, bm_hbm, st, pt,
+    p_hbm, m_hbm, a_hbm, b_hbm, or_hbm, an_hbm, bm_hbm, st_hbm, pt_hbm,
     out_p, out_m,
     P0, M0, A, B, OR, AN, BM, P1, M1, U1, V1, U0, V0,
-    KAP, JMP, MOV, JS0, W0, G0, K0,
+    KAP, JMP, MOV, JS0, W0, G0, K0, st, pt,
     load_sem, ss, rs,
 ):
     X, Y, Z = p_hbm.shape
@@ -60,6 +60,10 @@
         (bm_hbm, BM, 1), (a_hbm, A, 1), (b_hbm, B, 1),
     )):
         copy = pltpu.make_async_copy(src, dst.at[pl.ds(off, X), pl.ds(0, Y), :], load_sem.at[k])
+        copy.start()
+        loads.append(copy)
+    for k, (src, dst) in enumerate(((st_hbm, st), (pt_hbm, pt))):
+        copy = pltpu.make_async_copy(src, dst, load_sem.at[7 + k])
         copy.start()
         loads.append(copy)
 
@@ -150,13 +154,17 @@
     x_last = exchange("x", [x_layers(ref, 1, 1) for ref in (U0, V0)])
     y_last = exchange("y", [y_rows(ref, 1) for ref in (U0, V0)])
 
-    loads[0].wait()
-    loads[1].wait()
-    pl.semaphore_wait(barrier, count)
-    x_state[0]()
-    y_state[0]()
-    for copy in loads[2:]:
-        copy.wait()
+    with jax.named_scope("wait_load"):
+        loads[0].wait()
+        loads[1].wait()
+    with jax.named_scope("wait_barrier"):
+        pl.semaphore_wait(barrier, count)
+    with jax.named_scope("send_state"):
+        x_state[0]()
+        y_state[0]()
+    with jax.named_scope("wait_load_rest"):
+        for copy in loads[2:]:
+            copy.wait()
     x_rest[0]()
 
     lane = lax.broadcasted_iota(jnp.int32, (Y, Z), 1)
@@ -242,28 +250,44 @@
             return carry
         lax.fori_loop(low, high, step, 0)
 
-    over(0, X, tables)
-    y_state[1]()
+    with jax.named_scope("tables"):
+        over(0, X, tables)
+    with jax.named_scope("wait_y_state"):
+        y_state[1]()
     x_corner[0]()
-    over(1, X - 1, lambda x: forward(x, True))
-    x_state[1]()
-    over(0, 2, lambda k: forward(k * (X - 1), True))
-    y_middle[0]()
-    x_rest[1]()
-    x_corner[1]()
-    over(0, 2, lambda k: tables(k * (X + 1) - 1))
-    over(0, 2, lambda k: forward(k * (X + 1) - 1, False))
-    y_middle[1]()
-    over(0, 2, lambda k: backward(k * (X - 1)))
-    x_last[0]()
-    over(1, X - 1, backward)
-    y_last[0]()
-    y_last[1]()
-    over(1, X - 1, finish)
-    x_last[1]()
-    over(0, 2, lambda k: finish(k * (X - 1)))
-    for step in (x_state, y_state, x_rest, x_corner, y_middle, x_last, y_last):
-        step[2]()
+    with jax.named_scope("forward_inside"):
+        over(1, X - 1, lambda x: forward(x, True))
+    with jax.named_scope("wait_x_state"):
+        x_state[1]()
+    with jax.named_scope("forward_edge"):
+        over(0, 2, lambda k: forward(k * (X - 1), True))
+        y_middle[0]()
+    with jax.named_scope("wait_x_rest"):
+        x_rest[1]()
+    with jax.named_scope("wait_x_corner"):
+        x_corner[1]()
+    with jax.named_scope("forward_halo"):
+        over(0, 2, lambda k: tables(k * (X + 1) - 1))
+        over(0, 2, lambda k: forward(k * (X + 1) - 1, False))
+    with jax.named_scope("wait_y_middle"):
+        y_middle[1]()
+    with jax.named_scope("backward_edge"):
+        over(0, 2, lambda k: backward(k * (X - 1)))
+        x_last[0]()
+    with jax.named_scope("backward_inside"):
+        over(1, X - 1, backward)
+        y_last[0]()
+    with jax.named_scope("wait_y_last"):
+        y_last[1]()
+    with jax.named_scope("finish_inside"):
+        over(1, X - 1, finish)
+    with jax.named_scope("wait_x_last"):
+        x_last[1]()
+    with jax.named_scope("finish_edge"):
+        over(0, 2, lambda k: finish(k * (X - 1)))
+    with jax.named_scope("wait_sends"):
+        for step in (x_state, y_state, x_rest, x_corner, y_middle, x_last, y_last):
+            step[2]()
 
 
 def hand_over(p_ref, m_ref, p_out, m_out, sem):
@@ -281,14 +305,13 @@
     def on_device(*args):
         X, Y, Z = args[0].shape
         f32, i32 = jnp.float32, jnp.int32
-        anywhere = pl.BlockSpec(memory_space=pl.ANY)
-        scalars = pl.BlockSpec(memory_space=pltpu.SMEM)
+        hbm = pl.BlockSpec(memory_space=pltpu.HBM)
         vmem = pltpu.VMEM
         copies = 2 * (2 + 2 + 5 + 2 + 4 + 2 + 2)
         results = pl.pallas_call(
             functools.partial(kernel, nx_dev, ny_dev),
             out_shape=[vmem((X, Y, Z), f32)] * 2,
-            in_specs=[anywhere] * 7 + [scalars] * 2,
+            in_specs=[hbm] * 9,
             out_specs=[pl.BlockSpec(memory_space=vmem)] * 2,
             scratch_shapes=(
                 [vmem((X + 4, Y + 8, Z), f32)] * 2
@@ -297,19 +320,21 @@
                 + [vmem((X + 2, Y + 8, Z), f32)] * 6
                 + [vmem((X + 2, Y, Z), f32)] * 3
                 + [vmem((X, Y, Z), f32)] * 4
-                + [pltpu.SemaphoreType.DMA((7,))]
+                + [pltpu.SMEM(args[7].shape, f32), pltpu.SMEM(args[8].shape, f32)]
+                + [pltpu.SemaphoreType.DMA((9,))]
                 + [pltpu.SemaphoreType.DMA((copies,))] * 2
             ),
             compiler_params=pltpu.CompilerParams(
                 collective_id=0, has_side_effects=True, vmem_limit_bytes=32 * 1024 * 1024
             ),
             name="reverse",
-        )(*args)
+        )(*[pltpu.with_memory_space_constraint(arg, pltpu.HBM) for arg in args])
+        results = [pltpu.with_memory_space_constraint(r, vmem) for r in results]
         return pl.pallas_call(
             hand_over,
             out_shape=[jax.ShapeDtypeStruct((X, Y, Z), f32)] * 2,
             in_specs=[pl.BlockSpec(memory_space=vmem)] * 2,
-            out_specs=[anywhere] * 2,
+            out_specs=[hbm] * 2,
             scratch_shapes=[pltpu.SemaphoreType.DMA((2,))],
             name="hand_over",
         )(*results)

time: 44.9 us -> 32.4 us (0.72)
  local copies, waits for them, and re-layouts: 9.75 us -> 0 us
  Pallas kernels: 34.1 us -> 31.6 us
    unnamed x22 -> x0, local copies, waits for them, and re-layouts: 9.75 us -> none
    pallas_call x1, Pallas kernels: 32.1 us -> 30.7 us  [on_device(): pl.pallas_call(functools.partial(kernel, nx_dev, ny_dev), out_shape=[vmem...]
    pallas_call x1, Pallas kernels: 2 us -> 0.89 us  [on_device(): pl.pallas_call(hand_over, out_shape=[jax.ShapeDtypeStruct((X, Y, Z), f32)...]
where the time goes in v2:
time: 32.4 us; the launch traced here: 32.3 us
  Pallas kernels  31.6 us (98%)
  between operations  0.64 us (2%)
    pallas_call x1, Pallas kernels, on_device(): pl.pallas_call(functools.partial(kernel, nx_dev, ny_dev), out_shape=[vmem...  30.7 us
    pallas_call x1, Pallas kernels, on_device(): pl.pallas_call(hand_over, out_shape=[jax.ShapeDtypeStruct((X, Y, Z), f32)...  0.89 us

profile of v2, /device:TPU:34, one launch (start us, length us, event | category | flops | bytes accessed | tf_op | source)
XLA Modules:
  0.0 32.3 jit_solution(4136928416040003212)
XLA Ops:
  0.6 30.7 %reverse.1 = (f32[24,16,256]{2,1,0:T(8,128)S(1)}, f32[24,16,256]{2,1,0:T(8,128)S(1)}) custom-call(f32[24,16,256]{2,1,0:T(8,128)} %p_hbm.1, f32[24,16,256]{2,1,0:T(8,128)} %m_hbm.1, f32[24,16,256]{2,1,0:T(8,128)} %a_hbm.1, f32[24,16,256]{2,1,0:T(8,128)} %b_hbm.1, s32[24,16,256]{2,1,0:T(8,128)} %or_hbm.1, s32[24,16,256]{2,1,0:T(8,128)} %an_hbm.1, ...), custom_call_target="tpu_custom_call" | custom-call | tf_op jit(solution)/shard_map/reverse/pallas_call | solution.py:311
  31.4 0.9 %hand_over.1 = (f32[24,16,256]{2,1,0:T(8,128)}, f32[24,16,256]{2,1,0:T(8,128)}) custom-call(f32[24,16,256]{2,1,0:T(8,128)S(1)} %get-tuple-element.4.p_ref, f32[24,16,256]{2,1,0:T(8,128)S(1)} %get-tuple-element.5.m_ref), custom_call_target="tpu_custom_call" | custom-call | tf_op jit(solution)/shard_map/hand_over/pallas_call | solution.py:333

commit v3 on v2

v3 whole, which is shorter than its diff:
```python
import functools

import jax
import jax.numpy as jnp
from jax import lax
from jax.experimental import pallas as pl
from jax.experimental.pallas import tpu as pltpu
from jax.sharding import PartitionSpec as P

mobility_step = 0.1
well_height = 1.0
coupling = 1.0
diffusion_step = 0.03

MESH = pl.DeviceIdType.MESH


def pick(index, table, count):
    values = [table[k] for k in range(count)]
    bit = 1
    while len(values) > 1:
        odd = (index & bit) != 0
        values = [jnp.where(odd, values[k + 1], values[k]) for k in range(0, len(values), 2)]
        bit *= 2
    return values[0]


def local_terms(phase, jump):
    t = phase - phase * phase
    inverse = 1.0 / (1.0 - 2.0 * t)
    slope = 2.0 * t * inverse * inverse
    slope_derivative = 2.0 * (1.0 - 2.0 * phase) * (1.0 + 2.0 * t) * (inverse * inverse * inverse)
    release = 1.0 / (1.0 - jump * (phase * phase * inverse))
    return t, slope, slope_derivative, release


def kernel(
    nx_dev, ny_dev,
    p_hbm, m_hbm, a_hbm, b_hbm, or_hbm, an_hbm, bm_hbm, st_hbm, pt_hbm,
    out_p, out_m,
    A, B, OR, AN, BM, P0, M0, P1, M1, U1, V1, U0, V0, UD, VD, UU, VU,
    KAP, JMP, MOV, JS0, W0, G0, K0, st, pt,
    load_sem, ss, rs,
):
    X, Y, Z = p_hbm.shape
    HI, LO = Y, Y + 7
    gx, gy = lax.axis_index("gx"), lax.axis_index("gy")
    has = {
        ("x", 0): gx > 0, ("x", 1): gx < nx_dev - 1,
        ("y", 0): gy > 0, ("y", 1): gy < ny_dev - 1,
    }
    device = {
        ("x", 0): {"gx": gx - 1}, ("x", 1): {"gx": gx + 1},
        ("y", 0): {"gy": gy - 1}, ("y", 1): {"gy": gy + 1},
    }

    barrier = pltpu.get_barrier_semaphore()
    count = jnp.int32(0)
    for key, there in has.items():
        @pl.when(there)
        def _():
            pl.semaphore_signal(barrier, inc=1, device_id=device[key], device_id_type=MESH)
        count = count + there.astype(jnp.int32)

    rows = pl.ds(0, Y)
    loads = []
    for k, (src, dst) in enumerate((
        (p_hbm, P0.at[pl.ds(1, X), rows]), (m_hbm, M0.at[pl.ds(1, X), rows]),
        (an_hbm, AN), (or_hbm, OR), (bm_hbm, BM), (st_hbm, st), (pt_hbm, pt), (a_hbm, A), (b_hbm, B),
    )):
        copy = pltpu.make_async_copy(src, dst, load_sem.at[k])
        copy.start()
        loads.append(copy)

    sems = iter(range(ss.shape[0]))

    def exchange(axis, pieces):
        sends = {0: [], 1: []}
        arrivals = {0: [], 1: []}
        for down, down_to, up, up_to in pieces:
            for side, src, dst in ((0, down, down_to), (1, up, up_to)):
                k = next(sems)
                copy = pltpu.make_async_remote_copy(
                    src_ref=src, dst_ref=dst, send_sem=ss.at[k], recv_sem=rs.at[k],
                    device_id=device[axis, side], device_id_type=MESH,
                )
                sends[side].append(copy)
                arrivals[1 - side].append(copy)

        def each(groups, act):
            def run(sides=(0, 1)):
                for side in sides:
                    @pl.when(has[axis, side])
                    def _():
                        for copy in groups[side]:
                            act(copy)
            return run

        return (
            each(sends, lambda copy: copy.start()),
            each(arrivals, lambda copy: copy.wait_recv()),
            each(sends, lambda copy: copy.wait_send()),
        )

    def x_faces(ref):
        return ref.at[1, rows], ref.at[X + 1, rows], ref.at[X, rows], ref.at[0, rows]

    def y_faces(ref):
        own = pl.ds(1, X)
        return ref.at[own, 0], ref.at[own, HI], ref.at[own, Y - 1], ref.at[own, LO]

    def y_aside(ref, up, down):
        own = pl.ds(1, X)
        return ref.at[own, 0], up.at[:, 0], ref.at[own, Y - 1], down.at[:, 0]

    x_state = exchange("x", [
        (src.at[0], dst.at[X + 1, rows], src.at[X - 1], dst.at[0, rows]) for src, dst in ((p_hbm, P0), (m_hbm, M0))
    ])
    y_state = exchange("y", [y_faces(ref) for ref in (P0, M0)])
    x_middle = exchange("x", [x_faces(ref) for ref in (P1, M1, U1, V1)])
    y_middle = exchange("y", [y_faces(ref) for ref in (P1, M1, U1, V1)])
    x_last = exchange("x", [x_faces(ref) for ref in (U0, V0)])
    y_last = exchange("y", [y_aside(U0, UU, UD), y_aside(V0, VU, VD)])

    for side, layer in enumerate((0, X + 1)):
        @pl.when(jnp.logical_not(has["x", side]))
        def _():
            for ref in (P0, M0, P1, M1, U1, V1, U0, V0):
                ref[layer, :Y] = jnp.zeros((Y, Z), ref.dtype)
    for side, (row, aside) in enumerate(((LO, (UD, VD)), (HI, (UU, VU)))):
        @pl.when(jnp.logical_not(has["y", side]))
        def _():
            for ref in (P0, M0, P1, M1, U1, V1):
                ref[pl.ds(1, X), pl.ds(row, 1), :] = jnp.zeros((X, 1, Z), ref.dtype)
            for ref in aside:
                ref[:, pl.ds(0, 1), :] = jnp.zeros((X, 1, Z), ref.dtype)
    for ref in (U0, V0):
        ref[:, Y:, :] = jnp.zeros((X + 2, 8, Z), ref.dtype)

    with jax.named_scope("wait_barrier"):
        pl.semaphore_wait(barrier, count)
    x_state[0]()
    with jax.named_scope("wait_load"):
        loads[0].wait()
        loads[1].wait()
    y_state[0]()
    with jax.named_scope("wait_load_rest"):
        for copy in loads[2:]:
            copy.wait()

    lane = lax.broadcasted_iota(jnp.int32, (Y, Z), 1)
    first, last = lane == 0, lane == Z - 1

    def lap(ref, i, below=True, above=True):
        wide = ref[i]
        center = wide[:Y]
        beside = pltpu.roll(wide, Y + 7, 0)[:Y] + pltpu.roll(wide, 1, 0)[:Y]
        if below:
            beside = beside + ref[i - 1, :Y]
        if above:
            beside = beside + ref[i + 1, :Y]
        beside = beside + jnp.where(first, 0.0, pltpu.roll(center, 1, 1))
        beside = beside + jnp.where(last, 0.0, pltpu.roll(center, Z - 1, 1))
        return beside - 6.0 * center

    def tables(x):
        KAP[x] = pick(AN[x], st, st.shape[0])
        JMP[x] = 1.0 - pick(OR[x], pt, pt.shape[0])
        MOV[x] = 1.0 - BM[x].astype(jnp.float32)

    def forward(x):
        i = x + 1
        phase, potential = P0[i, :Y], M0[i, :Y]
        stiffness, jump, movable = KAP[x], JMP[x], MOV[x]
        t, slope, slope_derivative, release = local_terms(phase, jump)
        held_slope = jump * slope
        drive = (
            stiffness * lap(P0, i)
            - 2.0 * well_height * t * (1.0 - 2.0 * phase)
            + coupling * held_slope * potential
        )
        step = movable * mobility_step * drive
        flux = (diffusion_step * lap(M0, i) - held_slope * step) * release
        phase_next = phase + step
        P1[i, :Y] = phase_next
        M1[i, :Y] = potential + movable * flux
        JS0[x] = held_slope
        W0[x] = movable * release
        G0[x] = well_height * (12.0 * t - 2.0) + coupling * jump * slope_derivative * potential
        K0[x] = jump * (slope * flux - step * slope_derivative)
        _, slope, _, release = local_terms(phase_next, jump)
        spread = B[x] * (movable * release)
        pull = mobility_step * movable * (A[x] - spread * (jump * slope))
        U1[i, :Y] = stiffness * pull
        V1[i, :Y] = diffusion_step * spread

    def backward(x):
        i = x + 1
        phase, potential = P1[i, :Y], M1[i, :Y]
        stiffness, jump, movable = KAP[x], JMP[x], MOV[x]
        t, slope, slope_derivative, release = local_terms(phase, jump)
        held_slope = jump * slope
        drive = (
            stiffness * lap(P1, i)
            - 2.0 * well_height * t * (1.0 - 2.0 * phase)
            + coupling * held_slope * potential
        )
        step = movable * mobility_step * drive
        flux = (diffusion_step * lap(M1, i) - held_slope * step) * release
        gain = well_height * (12.0 * t - 2.0) + coupling * jump * slope_derivative * potential
        keep = jump * (slope * flux - step * slope_derivative)
        spread = B[x] * (movable * release)
        pull = mobility_step * movable * (A[x] - spread * held_slope)
        bar_p = A[x] + pull * gain + spread * keep + lap(U1, i)
        bar_m = B[x] + coupling * held_slope * pull + lap(V1, i)
        spread = bar_m * W0[x]
        pull = mobility_step * movable * (bar_p - spread * JS0[x])
        U0[i, :Y] = stiffness * pull
        V0[i, :Y] = diffusion_step * spread
        out_p[x] = bar_p + pull * G0[x] + spread * K0[x]
        out_m[x] = bar_m + coupling * JS0[x] * pull

    def finish(x, **sides):
        out_p[x] = out_p[x] + lap(U0, x + 1, **sides)
        out_m[x] = out_m[x] + lap(V0, x + 1, **sides)

    def finish_rows(x):
        for out, down, up in ((out_p, UD, UU), (out_m, VD, VU)):
            out[x, 0:1] = out[x, 0:1] + down[x, 0:1]
            out[x, Y - 1:Y] = out[x, Y - 1:Y] + up[x, 0:1]

    def over(low, high, body):
        def step(x, carry):
            body(x)
            return carry
        lax.fori_loop(low, high, step, 0, unroll=2)

    def edges(body):
        over(0, 2, lambda k: body(k * (X - 1)))

    with jax.named_scope("tables"):
        over(0, X, tables)
    with jax.named_scope("wait_y_state"):
        y_state[1]()
    with jax.named_scope("forward_inside"):
        over(1, X - 1, forward)
    with jax.named_scope("wait_x_state"):
        x_state[1]()
    with jax.named_scope("forward_edge"):
        edges(forward)
        x_middle[0]()
        y_middle[0]()
    with jax.named_scope("wait_middle"):
        y_middle[1]()
        x_middle[1]()
    with jax.named_scope("backward_edge"):
        edges(backward)
        x_last[0]()
    with jax.named_scope("backward_inside"):
        over(1, X - 1, backward)
        y_last[0]()
    with jax.named_scope("finish_inside"):
        over(1, X - 1, finish)
        finish(0, below=False)
        finish(X - 1, above=False)
    with jax.named_scope("wait_y_last"):
        y_last[1]()
        over(0, X, finish_rows)
    with jax.named_scope("wait_x_last"):
        x_last[1]()
        for x, layer in ((0, 0), (X - 1, X + 1)):
            out_p[x] = out_p[x] + U0[layer, :Y]
            out_m[x] = out_m[x] + V0[layer, :Y]
    with jax.named_scope("wait_sends"):
        for step in (x_state, y_state, x_middle, y_middle, x_last, y_last):
            step[2]()


def hand_over(p_ref, m_ref, p_out, m_out, sem):
    copies = [pltpu.make_async_copy(p_ref, p_out, sem.at[0]), pltpu.make_async_copy(m_ref, m_out, sem.at[1])]
    for copy in copies:
        copy.start()
    for copy in copies:
        copy.wait()


def solution(mesh):
    nx_dev, ny_dev = mesh.shape["gx"], mesh.shape["gy"]
    split = P("gx", "gy", None)

    def on_device(*args):
        X, Y, Z = args[0].shape
        f32, i32 = jnp.float32, jnp.int32
        hbm = pl.BlockSpec(memory_space=pltpu.HBM)
        vmem = pltpu.VMEM
        copies = 2 * 2 * (2 + 4 + 2)
        results = pl.pallas_call(
            functools.partial(kernel, nx_dev, ny_dev),
            out_shape=[vmem((X, Y, Z), f32)] * 2,
            in_specs=[hbm] * 9,
            out_specs=[pl.BlockSpec(memory_space=vmem)] * 2,
            scratch_shapes=(
                [vmem((X, Y, Z), f32)] * 2
                + [vmem((X, Y, Z), i32)] * 3
                + [vmem((X + 2, Y + 8, Z), f32)] * 8
                + [vmem((X, 8, Z), f32)] * 4
                + [vmem((X, Y, Z), f32)] * 7
                + [pltpu.SMEM(args[7].shape, f32), pltpu.SMEM(args[8].shape, f32)]
                + [pltpu.SemaphoreType.DMA((9,))]
                + [pltpu.SemaphoreType.DMA((copies,))] * 2
            ),
            compiler_params=pltpu.CompilerParams(
                collective_id=0, has_side_effects=True, vmem_limit_bytes=32 * 1024 * 1024
            ),
            name="reverse",
        )(*[pltpu.with_memory_space_constraint(arg, pltpu.HBM) for arg in args])
        results = [pltpu.with_memory_space_constraint(r, vmem) for r in results]
        return pl.pallas_call(
            hand_over,
            out_shape=[jax.ShapeDtypeStruct((X, Y, Z), f32)] * 2,
            in_specs=[pl.BlockSpec(memory_space=vmem)] * 2,
            out_specs=[hbm] * 2,
            scratch_shapes=[pltpu.SemaphoreType.DMA((2,))],
            name="hand_over",
        )(*results)

    return jax.shard_map(
        on_device, mesh=mesh, in_specs=(split,) * 7 + (P(), P()), out_specs=(split, split), check_vma=False
    )
```

time: 32.4 us -> 26.2 us (0.81)
  Pallas kernels: 31.6 us -> 25.2 us
    pallas_call x1, Pallas kernels: 30.7 us -> 24.3 us  [on_device(): pl.pallas_call(functools.partial(kernel, nx_dev, ny_dev), out_shape=[vmem...]
where the time goes in v3:
time: 26.2 us; the launch traced here: 25.8 us
  Pallas kernels  25.2 us (96%)
  between operations  0.64 us (2%)
    pallas_call x1, Pallas kernels, on_device(): pl.pallas_call(functools.partial(kernel, nx_dev, ny_dev), out_shape=[vmem...  24.3 us
    pallas_call x1, Pallas kernels, on_device(): pl.pallas_call(hand_over, out_shape=[jax.ShapeDtypeStruct((X, Y, Z), f32)...  0.89 us

profile of v3, /device:TPU:34, one launch (start us, length us, event | category | flops | bytes accessed | tf_op | source)
XLA Modules:
  0.0 25.8 jit_solution(17355050969729990501)
XLA Ops:
  0.6 24.3 %reverse.1 = (f32[24,16,256]{2,1,0:T(8,128)S(1)}, f32[24,16,256]{2,1,0:T(8,128)S(1)}) custom-call(f32[24,16,256]{2,1,0:T(8,128)} %p_hbm.1, f32[24,16,256]{2,1,0:T(8,128)} %m_hbm.1, f32[24,16,256]{2,1,0:T(8,128)} %a_hbm.1, f32[24,16,256]{2,1,0:T(8,128)} %b_hbm.1, s32[24,16,256]{2,1,0:T(8,128)} %or_hbm.1, s32[24,16,256]{2,1,0:T(8,128)} %an_hbm.1, ...), custom_call_target="tpu_custom_call" | custom-call | tf_op jit(solution)/shard_map/reverse/pallas_call | solution.py:297
  24.9 0.9 %hand_over.1 = (f32[24,16,256]{2,1,0:T(8,128)}, f32[24,16,256]{2,1,0:T(8,128)}) custom-call(f32[24,16,256]{2,1,0:T(8,128)S(1)} %get-tuple-element.4.p_ref, f32[24,16,256]{2,1,0:T(8,128)S(1)} %get-tuple-element.5.m_ref), custom_call_target="tpu_custom_call" | custom-call | tf_op jit(solution)/shard_map/hand_over/pallas_call | solution.py:318

commit v4 on v3

v4 whole, which is shorter than its diff:
```python
import functools

import jax
import jax.numpy as jnp
from jax import lax
from jax.experimental import pallas as pl
from jax.experimental.pallas import tpu as pltpu
from jax.sharding import PartitionSpec as P

mobility_step = 0.1
well_height = 1.0
coupling = 1.0
diffusion_step = 0.03

MESH = pl.DeviceIdType.MESH


def pick(index, table, count):
    values = [table[k] for k in range(count)]
    bit = 1
    while len(values) > 1:
        odd = (index & bit) != 0
        values = [jnp.where(odd, values[k + 1], values[k]) for k in range(0, len(values), 2)]
        bit *= 2
    return values[0]


def local_terms(phase, jump):
    t = phase - phase * phase
    denominator = 1.0 - 2.0 * t
    rest = denominator - jump * (phase - t)
    both = 1.0 / (denominator * rest)
    inverse = rest * both
    release = denominator * (denominator * both)
    square = inverse * inverse
    slope = 2.0 * t * square
    slope_derivative = (2.0 - 4.0 * phase) * (1.0 + 2.0 * t) * (square * inverse)
    return t, slope, slope_derivative, release


def kernel(
    nx_dev, ny_dev,
    p_hbm, m_hbm, a_hbm, b_hbm, or_hbm, an_hbm, bm_hbm, st_hbm, pt_hbm,
    out_p, out_m,
    A, B, OR, AN, BM, P0, M0, P1, M1, U1, V1, U0, V0, HP0, HM0, HP1, HM1, HU1, HV1, HU0, HV0,
    KAP, JMP, MOV, REACH, JS0, JD0, W0, G0, K0, JS1, JD1, W1, SP1, st, pt,
    load_sem, ss, rs,
):
    X, Y, Z = p_hbm.shape
    gx, gy = lax.axis_index("gx"), lax.axis_index("gy")
    has = {
        ("x", 0): gx > 0, ("x", 1): gx < nx_dev - 1,
        ("y", 0): gy > 0, ("y", 1): gy < ny_dev - 1,
    }
    device = {
        ("x", 0): {"gx": gx - 1}, ("x", 1): {"gx": gx + 1},
        ("y", 0): {"gy": gy - 1}, ("y", 1): {"gy": gy + 1},
    }

    barrier = pltpu.get_barrier_semaphore()
    count = jnp.int32(0)
    for key, there in has.items():
        @pl.when(there)
        def _():
            pl.semaphore_signal(barrier, inc=1, device_id=device[key], device_id_type=MESH)
        count = count + there.astype(jnp.int32)

    own = pl.ds(1, X)
    loads = []
    for k, (src, dst) in enumerate((
        (p_hbm, P0.at[own]), (m_hbm, M0.at[own]),
        (an_hbm, AN.at[own]), (or_hbm, OR.at[own]), (bm_hbm, BM.at[own]), (st_hbm, st), (pt_hbm, pt),
        (a_hbm, A.at[own]), (b_hbm, B.at[own]),
    )):
        copy = pltpu.make_async_copy(src, dst, load_sem.at[k])
        copy.start()
        loads.append(copy)

    sems = iter(range(ss.shape[0]))

    def exchange(axis, pieces):
        sends = {0: [], 1: []}
        arrivals = {0: [], 1: []}
        for down, down_to, up, up_to in pieces:
            for side, src, dst in ((0, down, down_to), (1, up, up_to)):
                k = next(sems)
                copy = pltpu.make_async_remote_copy(
                    src_ref=src, dst_ref=dst, send_sem=ss.at[k], recv_sem=rs.at[k],
                    device_id=device[axis, side], device_id_type=MESH,
                )
                sends[side].append(copy)
                arrivals[1 - side].append(copy)

        def each(groups, act):
            def run(sides=(0, 1)):
                for side in sides:
                    @pl.when(has[axis, side])
                    def _():
                        for copy in groups[side]:
                            act(copy)
            return run

        return (
            each(sends, lambda copy: copy.start()),
            each(arrivals, lambda copy: copy.wait_recv()),
            each(sends, lambda copy: copy.wait_send()),
        )

    def x_faces(ref):
        return ref.at[1], ref.at[X + 1], ref.at[X], ref.at[0]

    def y_faces(ref, aside):
        return ref.at[own, 0], aside.at[:, 7], ref.at[own, Y - 1], aside.at[:, 0]

    def x_given(src, dst):
        return src.at[0], dst.at[X + 1], src.at[X - 1], dst.at[0]

    x_state = exchange("x", [x_faces(P0), x_faces(M0)])
    x_given_rest = exchange("x", [
        x_given(src, dst) for src, dst in ((an_hbm, AN), (or_hbm, OR), (bm_hbm, BM), (a_hbm, A), (b_hbm, B))
    ])
    y_state = exchange("y", [y_faces(P0, HP0), y_faces(M0, HM0)])
    x_middle = exchange("x", [x_faces(ref) for ref in (P1, M1)])
    y_middle = exchange("y", [y_faces(P1, HP1), y_faces(M1, HM1), y_faces(U1, HU1), y_faces(V1, HV1)])
    x_last = exchange("x", [x_faces(ref) for ref in (U0, V0)])
    y_last = exchange("y", [y_faces(U0, HU0), y_faces(V0, HV0)])

    for side, layer in enumerate((0, X + 1)):
        @pl.when(jnp.logical_not(has["x", side]))
        def _():
            for ref in (P0, M0, P1, M1, U1, V1, U0, V0):
                ref[layer] = jnp.zeros((Y, Z), ref.dtype)

    with jax.named_scope("wait_barrier"):
        pl.semaphore_wait(barrier, count)
    pass
    with jax.named_scope("wait_load"):
        loads[0].wait()
        loads[1].wait()
    x_state[0]()
    y_state[0]()
    x_given_rest[0]()
    with jax.named_scope("wait_load_rest"):
        for copy in loads[2:]:
            copy.wait()

    lane = lax.broadcasted_iota(jnp.int32, (8, 128), 1)
    line = lax.broadcasted_iota(jnp.int32, (8, 128), 0)
    first_lane, last_lane, first_line, last_line = lane == 0, lane == 127, line == 0, line == 7

    def shifted(parts, by, size, axis, edge):
        turned = [pltpu.roll(part, by % size, axis) for part in parts]
        return [jnp.where(edge, before, here) for before, here in zip([0.0] + turned, turned)]

    def lap(ref, i, below=True, above=True):
        tiles = [[ref[i, a:a + 8, b:b + 128] for b in range(0, Z, 128)] for a in range(0, Y, 8)]
        result = []
        along_y = []
        for column in zip(*tiles):
            down = shifted(column, 1, 8, 0, first_line)
            up = shifted(column[::-1], -1, 8, 0, last_line)[::-1]
            along_y.append([d + u for d, u in zip(down, up)])
        for a, row in enumerate(tiles):
            left = shifted(row, 1, 128, 1, first_lane)
            right = shifted(row[::-1], -1, 128, 1, last_lane)[::-1]
            result.append(jnp.concatenate(
                [l + r + along_y[b][a] - 6.0 * c for b, (l, r, c) in enumerate(zip(left, right, row))], axis=1
            ))
        beside = jnp.concatenate(result, axis=0)
        if below:
            beside = beside + ref[i - 1]
        if above:
            beside = beside + ref[i + 1]
        return beside

    def tables(i):
        KAP[i] = pick(AN[i], st, st.shape[0])
        JMP[i] = 1.0 - pick(OR[i], pt, pt.shape[0])
        movable = 1.0 - BM[i].astype(jnp.float32)
        MOV[i] = movable
        REACH[i] = mobility_step * movable

    def sensitivities(at, phase):
        jump = JMP[at]
        _, slope, _, release = local_terms(phase, jump)
        spread = B[at] * (MOV[at] * release)
        U1[at] = KAP[at] * (REACH[at] * (A[at] - spread * (jump * slope)))
        V1[at] = diffusion_step * spread

    def forward(x):
        i = x + 1
        phase, potential = P0[i], M0[i]
        jump = JMP[i]
        t, slope, slope_derivative, release = local_terms(phase, jump)
        held_slope, held_derivative = jump * slope, jump * slope_derivative
        drive = (
            KAP[i] * lap(P0, i)
            - 2.0 * well_height * t * (1.0 - 2.0 * phase)
            + coupling * held_slope * potential
        )
        step = REACH[i] * drive
        yielding = MOV[i] * release
        flux = yielding * (diffusion_step * lap(M0, i) - held_slope * step)
        P1[i] = phase + step
        M1[i] = potential + flux
        JS0[x] = held_slope
        JD0[x] = held_derivative
        W0[x] = yielding
        G0[x] = well_height * (12.0 * t - 2.0) + coupling * held_derivative * potential
        K0[x] = held_slope * flux - held_derivative * step
        sensitivities(i, phase + step)

    def forward_row(x, row, aside):
        at, here, away = (x, slice(row, row + 1)), (x + 1, slice(row, row + 1)), (x, slice(aside, aside + 1))
        step = REACH[here] * KAP[here] * HP0[away]
        flux = W0[at] * (diffusion_step * HM0[away] - JS0[at] * step)
        phase = P1[here] + step
        P1[here] = phase
        M1[here] = M1[here] + flux
        K0[at] = K0[at] + JS0[at] * flux - JD0[at] * step
        sensitivities(here, phase)

    def backward(x):
        i = x + 1
        phase, potential = P1[i], M1[i]
        jump, reach = JMP[i], REACH[i]
        t, slope, slope_derivative, release = local_terms(phase, jump)
        held_slope, held_derivative = jump * slope, jump * slope_derivative
        drive = (
            KAP[i] * lap(P1, i)
            - 2.0 * well_height * t * (1.0 - 2.0 * phase)
            + coupling * held_slope * potential
        )
        step = reach * drive
        yielding = MOV[i] * release
        flux = yielding * (diffusion_step * lap(M1, i) - held_slope * step)
        gain = well_height * (12.0 * t - 2.0) + coupling * held_derivative * potential
        keep = held_slope * flux - held_derivative * step
        spread = B[i] * yielding
        pull = reach * (A[i] - spread * held_slope)
        JS1[x] = held_slope
        JD1[x] = held_derivative
        W1[x] = yielding
        SP1[x] = spread
        bar_p = A[i] + pull * gain + spread * keep + lap(U1, i)
        bar_m = B[i] + coupling * held_slope * pull + lap(V1, i)
        spread = bar_m * W0[x]
        pull = reach * (bar_p - spread * JS0[x])
        U0[i] = KAP[i] * pull
        V0[i] = diffusion_step * spread
        out_p[x] = bar_p + pull * G0[x] + spread * K0[x]
        out_m[x] = bar_m + coupling * JS0[x] * pull

    def backward_row(x, row, aside):
        at, here, away = (x, slice(row, row + 1)), (x + 1, slice(row, row + 1)), (x, slice(aside, aside + 1))
        step = REACH[here] * KAP[here] * HP1[away]
        flux = W1[at] * (diffusion_step * HM1[away] - JS1[at] * step)
        bar_p = SP1[at] * (JS1[at] * flux - JD1[at] * step) + HU1[away]
        bar_m = HV1[away]
        spread = bar_m * W0[at]
        pull = REACH[here] * (bar_p - spread * JS0[at])
        U0[here] = U0[here] + KAP[here] * pull
        V0[here] = V0[here] + diffusion_step * spread
        out_p[at] = out_p[at] + (bar_p + pull * G0[at] + spread * K0[at])
        out_m[at] = out_m[at] + (bar_m + coupling * JS0[at] * pull)

    def finish(x, **sides):
        out_p[x] = out_p[x] + lap(U0, x + 1, **sides)
        out_m[x] = out_m[x] + lap(V0, x + 1, **sides)

    def finish_row(x, row, aside):
        at, away = (x, slice(row, row + 1)), (x, slice(aside, aside + 1))
        out_p[at] = out_p[at] + HU0[away]
        out_m[at] = out_m[at] + HV0[away]

    def over(low, high, body, unroll=2):
        def step(x, carry):
            body(x)
            return carry
        lax.fori_loop(low, high, step, 0, unroll=unroll)

    def edges(body):
        over(0, 2, lambda k: body(k * (X - 1)))

    def by_rows(run, body):
        for side, row, aside in ((0, 0, 0), (1, Y - 1, 7)):
            @pl.when(has["y", side])
            def _():
                run(lambda x: body(x, row, aside))

    def inside_rows(body):
        by_rows(lambda act: over(1, X - 1, act, 2), body)

    def edge_rows(body):
        by_rows(edges, body)

    with jax.named_scope("tables"):
        over(1, X + 1, tables)
    with jax.named_scope("forward_inside"):
        over(1, X - 1, forward)
    with jax.named_scope("forward_edges"):
        y_state[1]()
        x_state[1]()
        edges(forward)
        edge_rows(forward_row)
        x_middle[0]()
    with jax.named_scope("forward_rows"):
        inside_rows(forward_row)
        y_middle[0]()
    with jax.named_scope("backward_inside"):
        x_given_rest[1]()
        over(0, 2, lambda k: tables(k * (X + 1)))
        over(1, X - 1, backward)
    with jax.named_scope("backward_edges"):
        y_middle[1]()
        x_middle[1]()
        for side, layer in enumerate((0, X + 1)):
            @pl.when(has["x", side])
            def _():
                sensitivities(layer, P1[layer])
        edges(backward)
        edge_rows(backward_row)
        x_last[0]()
    with jax.named_scope("backward_rows"):
        inside_rows(backward_row)
        y_last[0]()
    with jax.named_scope("finish_inside"):
        over(1, X - 1, finish)
        finish(0, below=False)
        finish(X - 1, above=False)
    with jax.named_scope("finish_rows"):
        y_last[1]()
        by_rows(lambda act: over(0, X, act, 4), finish_row)
    with jax.named_scope("finish_edges"):
        x_last[1]()
        for x, layer in ((0, 0), (X - 1, X + 1)):
            out_p[x] = out_p[x] + U0[layer]
            out_m[x] = out_m[x] + V0[layer]
    with jax.named_scope("wait_sends"):
        for step in (x_state, y_state, x_given_rest, x_middle, y_middle, x_last, y_last):
            step[2]()


def hand_over(p_ref, m_ref, p_out, m_out, sem):
    copies = [pltpu.make_async_copy(p_ref, p_out, sem.at[0]), pltpu.make_async_copy(m_ref, m_out, sem.at[1])]
    for copy in copies:
        copy.start()
    for copy in copies:
        copy.wait()


def solution(mesh):
    nx_dev, ny_dev = mesh.shape["gx"], mesh.shape["gy"]
    split = P("gx", "gy", None)

    def on_device(*args):
        X, Y, Z = args[0].shape
        f32, i32 = jnp.float32, jnp.int32
        hbm = pl.BlockSpec(memory_space=pltpu.HBM)
        vmem = pltpu.VMEM
        copies = 2 * (2 + 5 + 2 + 2) + 2 * (2 + 4 + 2)
        results = pl.pallas_call(
            functools.partial(kernel, nx_dev, ny_dev),
            out_shape=[vmem((X, Y, Z), f32)] * 2,
            in_specs=[hbm] * 9,
            out_specs=[pl.BlockSpec(memory_space=vmem)] * 2,
            scratch_shapes=(
                [vmem((X + 2, Y, Z), f32)] * 2
                + [vmem((X + 2, Y, Z), i32)] * 3
                + [vmem((X + 2, Y, Z), f32)] * 8
                + [vmem((X, 8, Z), f32)] * 8
                + [vmem((X + 2, Y, Z), f32)] * 4
                + [vmem((X, Y, Z), f32)] * 9
                + [pltpu.SMEM(args[7].shape, f32), pltpu.SMEM(args[8].shape, f32)]
                + [pltpu.SemaphoreType.DMA((9,))]
                + [pltpu.SemaphoreType.DMA((copies,))] * 2
            ),
            compiler_params=pltpu.CompilerParams(
                collective_id=0, has_side_effects=True, vmem_limit_bytes=32 * 1024 * 1024
            ),
            name="reverse",
        )(*[pltpu.with_memory_space_constraint(arg, pltpu.HBM) for arg in args])
        results = [pltpu.with_memory_space_constraint(r, vmem) for r in results]
        return pl.pallas_call(
            hand_over,
            out_shape=[jax.ShapeDtypeStruct((X, Y, Z), f32)] * 2,
            in_specs=[pl.BlockSpec(memory_space=vmem)] * 2,
            out_specs=[hbm] * 2,
            scratch_shapes=[pltpu.SemaphoreType.DMA((2,))],
            name="hand_over",
        )(*results)

    return jax.shard_map(
        on_device, mesh=mesh, in_specs=(split,) * 7 + (P(), P()), out_specs=(split, split), check_vma=False
    )
```

time: 26.2 us -> 25.1 us (0.958)
  Pallas kernels: 25.2 us -> 24.3 us
    pallas_call x1, Pallas kernels: 24.3 us -> 23.4 us  [on_device(): pl.pallas_call(functools.partial(kernel, nx_dev, ny_dev), out_shape=[vmem...]
where the time goes in v4:
time: 25.1 us; the launch traced here: 25 us
  Pallas kernels  24.3 us (97%)
  between operations  0.64 us (3%)
    pallas_call x1, Pallas kernels, on_device(): pl.pallas_call(functools.partial(kernel, nx_dev, ny_dev), out_shape=[vmem...  23.4 us
    pallas_call x1, Pallas kernels, on_device(): pl.pallas_call(hand_over, out_shape=[jax.ShapeDtypeStruct((X, Y, Z), f32)...  0.89 us

profile of v4, /device:TPU:34, one launch (start us, length us, event | category | flops | bytes accessed | tf_op | source)
XLA Modules:
  0.0 25.0 jit_solution(3323132542474363218)
XLA Ops:
  0.6 23.4 %reverse.1 = (f32[24,16,256]{2,1,0:T(8,128)S(1)}, f32[24,16,256]{2,1,0:T(8,128)S(1)}) custom-call(f32[24,16,256]{2,1,0:T(8,128)} %p_hbm.1, f32[24,16,256]{2,1,0:T(8,128)} %m_hbm.1, f32[24,16,256]{2,1,0:T(8,128)} %a_hbm.1, f32[24,16,256]{2,1,0:T(8,128)} %b_hbm.1, s32[24,16,256]{2,1,0:T(8,128)} %or_hbm.1, s32[24,16,256]{2,1,0:T(8,128)} %an_hbm.1, ...), custom_call_target="tpu_custom_call" | custom-call | tf_op jit(solution)/shard_map/reverse/pallas_call | solution.py:362
  24.1 0.9 %hand_over.1 = (f32[24,16,256]{2,1,0:T(8,128)}, f32[24,16,256]{2,1,0:T(8,128)}) custom-call(f32[24,16,256]{2,1,0:T(8,128)S(1)} %get-tuple-element.4.p_ref, f32[24,16,256]{2,1,0:T(8,128)S(1)} %get-tuple-element.5.m_ref), custom_call_target="tpu_custom_call" | custom-call | tf_op jit(solution)/shard_map/hand_over/pallas_call | solution.py:384

commit v5 on v4

--- a/solution.py
+++ b/solution.py
@@ -42,7 +42,7 @@
     nx_dev, ny_dev,
     p_hbm, m_hbm, a_hbm, b_hbm, or_hbm, an_hbm, bm_hbm, st_hbm, pt_hbm,
     out_p, out_m,
-    A, B, OR, AN, BM, P0, M0, P1, M1, U1, V1, U0, V0, HP0, HM0, HP1, HM1, HU1, HV1, HU0, HV0,
+    A, B, OR, AN, BM, P0, M0, P1, M1, U1, V1, U0, V0, CO, CI, HP0, HM0, HP1, HM1, HU1, HV1, HU0, HV0,
     KAP, JMP, MOV, REACH, JS0, JD0, W0, G0, K0, JS1, JD1, W1, SP1, st, pt,
     load_sem, ss, rs,
 ):
@@ -78,7 +78,9 @@
 
     sems = iter(range(ss.shape[0]))
 
-    def exchange(axis, pieces):
+    def exchange(axis, pieces, send_if=None, arrive_if=None):
+        there = {side: has[axis, side] for side in (0, 1)}
+        send_if, arrive_if = send_if or there, arrive_if or there
         sends = {0: [], 1: []}
         arrivals = {0: [], 1: []}
         for down, down_to, up, up_to in pieces:
@@ -91,37 +93,35 @@
                 sends[side].append(copy)
                 arrivals[1 - side].append(copy)
 
-        def each(groups, act):
-            def run(sides=(0, 1)):
-                for side in sides:
-                    @pl.when(has[axis, side])
-                    def _():
-                        for copy in groups[side]:
-                            act(copy)
+        def each(groups, conditions, act):
+            def run():
+                for side in (0, 1):
+                    if groups[side]:
+                        @pl.when(conditions[side])
+                        def _():
+                            for copy in groups[side]:
+                                act(copy)
             return run
 
         return (
-            each(sends, lambda copy: copy.start()),
-            each(arrivals, lambda copy: copy.wait_recv()),
-            each(sends, lambda copy: copy.wait_send()),
+            each(sends, send_if, lambda copy: copy.start()),
+            each(arrivals, arrive_if, lambda copy: copy.wait_recv()),
+            each(sends, send_if, lambda copy: copy.wait_send()),
         )
 
     def x_faces(ref):
         return ref.at[1], ref.at[X + 1], ref.at[X], ref.at[0]
 
-    def y_faces(ref, aside):
-        return ref.at[own, 0], aside.at[:, 7], ref.at[own, Y - 1], aside.at[:, 0]
-
-    def x_given(src, dst):
-        return src.at[0], dst.at[X + 1], src.at[X - 1], dst.at[0]
+    inside = pl.ds(2, X - 2)
+
+    def y_faces(ref, aside, layers=own):
+        return ref.at[layers, 0], aside.at[layers, 7], ref.at[layers, Y - 1], aside.at[layers, 0]
 
     x_state = exchange("x", [x_faces(P0), x_faces(M0)])
-    x_given_rest = exchange("x", [
-        x_given(src, dst) for src, dst in ((an_hbm, AN), (or_hbm, OR), (bm_hbm, BM), (a_hbm, A), (b_hbm, B))
-    ])
     y_state = exchange("y", [y_faces(P0, HP0), y_faces(M0, HM0)])
-    x_middle = exchange("x", [x_faces(ref) for ref in (P1, M1)])
-    y_middle = exchange("y", [y_faces(P1, HP1), y_faces(M1, HM1), y_faces(U1, HU1), y_faces(V1, HV1)])
+    x_middle = exchange("x", [x_faces(ref) for ref in (P1, M1, U1, V1)])
+    y_edge = exchange("y", [(CO.at[0], CI.at[1], CO.at[1], CI.at[0])])
+    y_middle = exchange("y", [y_faces(P1, HP1, inside), y_faces(M1, HM1, inside), y_faces(U1, HU1, inside), y_faces(V1, HV1, inside)])
     x_last = exchange("x", [x_faces(ref) for ref in (U0, V0)])
     y_last = exchange("y", [y_faces(U0, HU0), y_faces(V0, HV0)])
 
@@ -139,7 +139,6 @@
         loads[1].wait()
     x_state[0]()
     y_state[0]()
-    x_given_rest[0]()
     with jax.named_scope("wait_load_rest"):
         for copy in loads[2:]:
             copy.wait()
@@ -187,8 +186,7 @@
         U1[at] = KAP[at] * (REACH[at] * (A[at] - spread * (jump * slope)))
         V1[at] = diffusion_step * spread
 
-    def forward(x):
-        i = x + 1
+    def forward(i):
         phase, potential = P0[i], M0[i]
         jump = JMP[i]
         t, slope, slope_derivative, release = local_terms(phase, jump)
@@ -203,25 +201,25 @@
         flux = yielding * (diffusion_step * lap(M0, i) - held_slope * step)
         P1[i] = phase + step
         M1[i] = potential + flux
-        JS0[x] = held_slope
-        JD0[x] = held_derivative
-        W0[x] = yielding
-        G0[x] = well_height * (12.0 * t - 2.0) + coupling * held_derivative * potential
-        K0[x] = held_slope * flux - held_derivative * step
+        JS0[i] = held_slope
+        JD0[i] = held_derivative
+        W0[i] = yielding
+        G0[i] = well_height * (12.0 * t - 2.0) + coupling * held_derivative * potential
+        K0[i] = held_slope * flux - held_derivative * step
         sensitivities(i, phase + step)
 
-    def forward_row(x, row, aside):
-        at, here, away = (x, slice(row, row + 1)), (x + 1, slice(row, row + 1)), (x, slice(aside, aside + 1))
+    def forward_row(i, row, aside):
+        here, away = (i, slice(row, row + 1)), (i, slice(aside, aside + 1))
         step = REACH[here] * KAP[here] * HP0[away]
-        flux = W0[at] * (diffusion_step * HM0[away] - JS0[at] * step)
+        flux = W0[here] * (diffusion_step * HM0[away] - JS0[here] * step)
         phase = P1[here] + step
         P1[here] = phase
         M1[here] = M1[here] + flux
-        K0[at] = K0[at] + JS0[at] * flux - JD0[at] * step
+        K0[here] = K0[here] + JS0[here] * flux - JD0[here] * step
         sensitivities(here, phase)
 
-    def backward(x):
-        i = x + 1
+    def backward(i):
+        x = i - 1
         phase, potential = P1[i], M1[i]
         jump, reach = JMP[i], REACH[i]
         t, slope, slope_derivative, release = local_terms(phase, jump)
@@ -238,38 +236,38 @@
         keep = held_slope * flux - held_derivative * step
         spread = B[i] * yielding
         pull = reach * (A[i] - spread * held_slope)
-        JS1[x] = held_slope
-        JD1[x] = held_derivative
-        W1[x] = yielding
-        SP1[x] = spread
+        JS1[i] = held_slope
+        JD1[i] = held_derivative
+        W1[i] = yielding
+        SP1[i] = spread
         bar_p = A[i] + pull * gain + spread * keep + lap(U1, i)
         bar_m = B[i] + coupling * held_slope * pull + lap(V1, i)
-        spread = bar_m * W0[x]
-        pull = reach * (bar_p - spread * JS0[x])
+        spread = bar_m * W0[i]
+        pull = reach * (bar_p - spread * JS0[i])
         U0[i] = KAP[i] * pull
         V0[i] = diffusion_step * spread
-        out_p[x] = bar_p + pull * G0[x] + spread * K0[x]
-        out_m[x] = bar_m + coupling * JS0[x] * pull
-
-    def backward_row(x, row, aside):
-        at, here, away = (x, slice(row, row + 1)), (x + 1, slice(row, row + 1)), (x, slice(aside, aside + 1))
+        out_p[x] = bar_p + pull * G0[i] + spread * K0[i]
+        out_m[x] = bar_m + coupling * JS0[i] * pull
+
+    def backward_row(i, row, aside):
+        at, here, away = (i - 1, slice(row, row + 1)), (i, slice(row, row + 1)), (i, slice(aside, aside + 1))
         step = REACH[here] * KAP[here] * HP1[away]
-        flux = W1[at] * (diffusion_step * HM1[away] - JS1[at] * step)
-        bar_p = SP1[at] * (JS1[at] * flux - JD1[at] * step) + HU1[away]
+        flux = W1[here] * (diffusion_step * HM1[away] - JS1[here] * step)
+        bar_p = SP1[here] * (JS1[here] * flux - JD1[here] * step) + HU1[away]
         bar_m = HV1[away]
-        spread = bar_m * W0[at]
-        pull = REACH[here] * (bar_p - spread * JS0[at])
+        spread = bar_m * W0[here]
+        pull = REACH[here] * (bar_p - spread * JS0[here])
         U0[here] = U0[here] + KAP[here] * pull
         V0[here] = V0[here] + diffusion_step * spread
-        out_p[at] = out_p[at] + (bar_p + pull * G0[at] + spread * K0[at])
-        out_m[at] = out_m[at] + (bar_m + coupling * JS0[at] * pull)
-
-    def finish(x, **sides):
-        out_p[x] = out_p[x] + lap(U0, x + 1, **sides)
-        out_m[x] = out_m[x] + lap(V0, x + 1, **sides)
-
-    def finish_row(x, row, aside):
-        at, away = (x, slice(row, row + 1)), (x, slice(aside, aside + 1))
+        out_p[at] = out_p[at] + (bar_p + pull * G0[here] + spread * K0[here])
+        out_m[at] = out_m[at] + (bar_m + coupling * JS0[here] * pull)
+
+    def finish(i, **sides):
+        out_p[i - 1] = out_p[i - 1] + lap(U0, i, **sides)
+        out_m[i - 1] = out_m[i - 1] + lap(V0, i, **sides)
+
+    def finish_row(i, row, aside):
+        at, away = (i - 1, slice(row, row + 1)), (i, slice(aside, aside + 1))
         out_p[at] = out_p[at] + HU0[away]
         out_m[at] = out_m[at] + HV0[away]
 
@@ -280,7 +278,7 @@
         lax.fori_loop(low, high, step, 0, unroll=unroll)
 
     def edges(body):
-        over(0, 2, lambda k: body(k * (X - 1)))
+        over(0, 2, lambda k: body(1 + k * (X - 1)))
 
     def by_rows(run, body):
         for side, row, aside in ((0, 0, 0), (1, Y - 1, 7)):
@@ -289,55 +287,65 @@
                 run(lambda x: body(x, row, aside))
 
     def inside_rows(body):
-        by_rows(lambda act: over(1, X - 1, act, 2), body)
+        by_rows(lambda act: over(2, X, act, 2), body)
 
     def edge_rows(body):
         by_rows(edges, body)
+
+    def corners(*refs):
+        return [(ref, layer) for ref in refs for layer in (1, X)]
 
     with jax.named_scope("tables"):
         over(1, X + 1, tables)
     with jax.named_scope("forward_inside"):
-        over(1, X - 1, forward)
+        over(2, X, forward)
+    def forward_rows():
+        inside_rows(forward_row)
+        y_middle[0]()
+
+    y_state[1]()
     with jax.named_scope("forward_edges"):
-        y_state[1]()
         x_state[1]()
         edges(forward)
         edge_rows(forward_row)
         x_middle[0]()
-    with jax.named_scope("forward_rows"):
-        inside_rows(forward_row)
-        y_middle[0]()
+        for side, row in ((0, 0), (1, Y - 1)):
+            for k, (ref, layer) in enumerate(corners(P1, M1, U1, V1)):
+                CO[side, k:k + 1] = ref[layer, row:row + 1]
+        y_edge[0]()
+    with jax.named_scope("forward_rows_late"):
+        forward_rows()
     with jax.named_scope("backward_inside"):
-        x_given_rest[1]()
-        over(0, 2, lambda k: tables(k * (X + 1)))
-        over(1, X - 1, backward)
+        over(2, X, backward)
     with jax.named_scope("backward_edges"):
-        y_middle[1]()
+        y_edge[1]()
+        for side, aside in ((0, 0), (1, 7)):
+            @pl.when(has["y", side])
+            def _():
+                for k, (ref, layer) in enumerate(corners(HP1, HM1, HU1, HV1)):
+                    ref[layer, aside:aside + 1] = CI[side, k:k + 1]
         x_middle[1]()
-        for side, layer in enumerate((0, X + 1)):
-            @pl.when(has["x", side])
-            def _():
-                sensitivities(layer, P1[layer])
         edges(backward)
         edge_rows(backward_row)
         x_last[0]()
     with jax.named_scope("backward_rows"):
+        y_middle[1]()
         inside_rows(backward_row)
         y_last[0]()
     with jax.named_scope("finish_inside"):
-        over(1, X - 1, finish)
-        finish(0, below=False)
-        finish(X - 1, above=False)
+        over(2, X, finish)
+        finish(1, below=False)
+        finish(X, above=False)
     with jax.named_scope("finish_rows"):
         y_last[1]()
-        by_rows(lambda act: over(0, X, act, 4), finish_row)
+        by_rows(lambda act: over(1, X + 1, act, 4), finish_row)
     with jax.named_scope("finish_edges"):
         x_last[1]()
         for x, layer in ((0, 0), (X - 1, X + 1)):
             out_p[x] = out_p[x] + U0[layer]
             out_m[x] = out_m[x] + V0[layer]
     with jax.named_scope("wait_sends"):
-        for step in (x_state, y_state, x_given_rest, x_middle, y_middle, x_last, y_last):
+        for step in (x_state, y_state, x_middle, y_edge, y_middle, x_last, y_last):
             step[2]()
 
 
@@ -358,7 +366,7 @@
         f32, i32 = jnp.float32, jnp.int32
         hbm = pl.BlockSpec(memory_space=pltpu.HBM)
         vmem = pltpu.VMEM
-        copies = 2 * (2 + 5 + 2 + 2) + 2 * (2 + 4 + 2)
+        copies = 2 * (2 + 4 + 2) + 2 * (2 + 1 + 4 + 2)
         results = pl.pallas_call(
             functools.partial(kernel, nx_dev, ny_dev),
             out_shape=[vmem((X, Y, Z), f32)] * 2,
@@ -368,9 +376,9 @@
                 [vmem((X + 2, Y, Z), f32)] * 2
                 + [vmem((X + 2, Y, Z), i32)] * 3
                 + [vmem((X + 2, Y, Z), f32)] * 8
-                + [vmem((X, 8, Z), f32)] * 8
-                + [vmem((X + 2, Y, Z), f32)] * 4
-                + [vmem((X, Y, Z), f32)] * 9
+                + [vmem((2, 8, Z), f32)] * 2
+                + [vmem((X + 2, 8, Z), f32)] * 8
+                + [vmem((X + 2, Y, Z), f32)] * 13
                 + [pltpu.SMEM(args[7].shape, f32), pltpu.SMEM(args[8].shape, f32)]
                 + [pltpu.SemaphoreType.DMA((9,))]
                 + [pltpu.SemaphoreType.DMA((copies,))] * 2

time: 25.1 us -> 24.4 us (0.972)
  the two profiles are of different devices: /device:TPU:34 before, /device:TPU:23 now
where the time goes in v5:
time: 24.4 us; the launch traced here: 24.3 us
  Pallas kernels  23.7 us (97%)
  between operations  0.64 us (3%)
    pallas_call x1, Pallas kernels, on_device(): pl.pallas_call(functools.partial(kernel, nx_dev, ny_dev), out_shape=[vmem...  22.8 us
    pallas_call x1, Pallas kernels, on_device(): pl.pallas_call(hand_over, out_shape=[jax.ShapeDtypeStruct((X, Y, Z), f32)...  0.89 us

profile of v5, /device:TPU:23, one launch (start us, length us, event | category | flops | bytes accessed | tf_op | source)
XLA Modules:
  0.0 24.3 jit_solution(15624672636384806896)
XLA Ops:
  0.6 22.8 %reverse.1 = (f32[24,16,256]{2,1,0:T(8,128)S(1)}, f32[24,16,256]{2,1,0:T(8,128)S(1)}) custom-call(f32[24,16,256]{2,1,0:T(8,128)} %p_hbm.1, f32[24,16,256]{2,1,0:T(8,128)} %m_hbm.1, f32[24,16,256]{2,1,0:T(8,128)} %a_hbm.1, f32[24,16,256]{2,1,0:T(8,128)} %b_hbm.1, s32[24,16,256]{2,1,0:T(8,128)} %or_hbm.1, s32[24,16,256]{2,1,0:T(8,128)} %an_hbm.1, ...), custom_call_target="tpu_custom_call" | custom-call | tf_op jit(solution)/shard_map/reverse/pallas_call | solution.py:370
  23.4 0.9 %hand_over.1 = (f32[24,16,256]{2,1,0:T(8,128)}, f32[24,16,256]{2,1,0:T(8,128)}) custom-call(f32[24,16,256]{2,1,0:T(8,128)S(1)} %get-tuple-element.4.p_ref, f32[24,16,256]{2,1,0:T(8,128)S(1)} %get-tuple-element.5.m_ref), custom_call_target="tpu_custom_call" | custom-call | tf_op jit(solution)/shard_map/hand_over/pallas_call | solution.py:392

commit v6 on v5

--- a/solution.py
+++ b/solution.py
@@ -13,6 +13,7 @@
 diffusion_step = 0.03
 
 MESH = pl.DeviceIdType.MESH
+RUN = 4
 
 
 def pick(index, table, count):
@@ -42,9 +43,9 @@
     nx_dev, ny_dev,
     p_hbm, m_hbm, a_hbm, b_hbm, or_hbm, an_hbm, bm_hbm, st_hbm, pt_hbm,
     out_p, out_m,
-    A, B, OR, AN, BM, P0, M0, P1, M1, U1, V1, U0, V0, CO, CI, HP0, HM0, HP1, HM1, HU1, HV1, HU0, HV0,
+    A, B, OR, AN, BM, P0, M0, P1, M1, U1, V1, U0, V0, CO, CI, DO, DI, HP0, HM0, HP1, HM1, HU1, HV1, HU0, HV0,
     KAP, JMP, MOV, REACH, JS0, JD0, W0, G0, K0, JS1, JD1, W1, SP1, st, pt,
-    load_sem, ss, rs,
+    load_sem, ss, rs, ready,
 ):
     X, Y, Z = p_hbm.shape
     gx, gy = lax.axis_index("gx"), lax.axis_index("gy")
@@ -57,13 +58,28 @@
         ("y", 0): {"gy": gy - 1}, ("y", 1): {"gy": gy + 1},
     }
 
+    at, even = lax.rem(gx, RUN), lax.rem(gy, 2) == 0
+    odd, begins, ends = jnp.logical_not(even), at == 0, at == RUN - 1
+    mutual = {("x", 0): has["x", 0] & begins & odd, ("x", 1): has["x", 1] & ends & odd}
+    caller = begins ^ even
+    calls = {
+        ("x", 0): has["x", 0] & (begins | ends), ("x", 1): (has["x", 1] & (at < 2)) | mutual["x", 1],
+        ("y", 0): has["y", 0] & caller, ("y", 1): has["y", 1] & caller,
+    }
+    called = {key: has[key] & jnp.logical_not(calls[key]) for key in has}
+    asks = dict(calls)
+    asks["x", 0] = calls["x", 0] & jnp.logical_not(mutual["x", 0])
+    asks["x", 1] = calls["x", 1] & jnp.logical_not(mutual["x", 1])
+    answer = {key: k for k, key in enumerate(has)}
+
     barrier = pltpu.get_barrier_semaphore()
     count = jnp.int32(0)
-    for key, there in has.items():
-        @pl.when(there)
+    for key in has:
+        @pl.when(calls[key])
         def _():
             pl.semaphore_signal(barrier, inc=1, device_id=device[key], device_id_type=MESH)
-        count = count + there.astype(jnp.int32)
+        count = count + called[key].astype(jnp.int32)
+    count = count + mutual["x", 1].astype(jnp.int32)
 
     own = pl.ds(1, X)
     loads = []
@@ -94,13 +110,12 @@
                 arrivals[1 - side].append(copy)
 
         def each(groups, conditions, act):
-            def run():
-                for side in (0, 1):
-                    if groups[side]:
-                        @pl.when(conditions[side])
-                        def _():
-                            for copy in groups[side]:
-                                act(copy)
+            def run(sides=(0, 1)):
+                for side in sides:
+                    @pl.when(conditions[side])
+                    def _():
+                        for copy in groups[side]:
+                            act(copy)
             return run
 
         return (
@@ -117,13 +132,16 @@
     def y_faces(ref, aside, layers=own):
         return ref.at[layers, 0], aside.at[layers, 7], ref.at[layers, Y - 1], aside.at[layers, 0]
 
-    x_state = exchange("x", [x_faces(P0), x_faces(M0)])
+    x_state = exchange("x", [
+        (ref.at[1], ref.at[X + 1], src.at[X - 1], ref.at[0]) for src, ref in ((p_hbm, P0), (m_hbm, M0))
+    ])
     y_state = exchange("y", [y_faces(P0, HP0), y_faces(M0, HM0)])
     x_middle = exchange("x", [x_faces(ref) for ref in (P1, M1, U1, V1)])
     y_edge = exchange("y", [(CO.at[0], CI.at[1], CO.at[1], CI.at[0])])
     y_middle = exchange("y", [y_faces(P1, HP1, inside), y_faces(M1, HM1, inside), y_faces(U1, HU1, inside), y_faces(V1, HV1, inside)])
     x_last = exchange("x", [x_faces(ref) for ref in (U0, V0)])
-    y_last = exchange("y", [y_faces(U0, HU0), y_faces(V0, HV0)])
+    y_last = exchange("y", [y_faces(U0, HU0, inside), y_faces(V0, HV0, inside)])
+    y_last_edge = exchange("y", [(DO.at[0], DI.at[1], DO.at[1], DI.at[0])])
 
     for side, layer in enumerate((0, X + 1)):
         @pl.when(jnp.logical_not(has["x", side]))
@@ -131,17 +149,32 @@
             for ref in (P0, M0, P1, M1, U1, V1, U0, V0):
                 ref[layer] = jnp.zeros((Y, Z), ref.dtype)
 
-    with jax.named_scope("wait_barrier"):
-        pl.semaphore_wait(barrier, count)
-    pass
-    with jax.named_scope("wait_load"):
-        loads[0].wait()
-        loads[1].wait()
-    x_state[0]()
-    y_state[0]()
-    with jax.named_scope("wait_load_rest"):
-        for copy in loads[2:]:
-            copy.wait()
+    pl.when(count > 0)(lambda: pl.semaphore_wait(barrier, count))
+    for axis, side in has:
+        @pl.when(called[axis, side])
+        def _():
+            pl.semaphore_signal(
+                ready.at[answer[axis, 1 - side]], inc=1, device_id=device[axis, side], device_id_type=MESH
+            )
+
+    def wait_answer(key):
+        pl.semaphore_wait(ready.at[answer[key]], 1)
+
+    pl.when(called["x", 1] | mutual["x", 1])(lambda: x_state[0]((1,)))
+    loads[0].wait()
+    loads[1].wait()
+    pl.when(called["x", 0])(lambda: x_state[0]((0,)))
+    for side in (0, 1):
+        pl.when(asks["y", side])(lambda: wait_answer(("y", side)))
+        y_state[0]((side,))
+
+    @pl.when(asks["x", 0] & ends)
+    def _():
+        wait_answer(("x", 0))
+        x_state[0]((0,))
+
+    for copy in loads[2:]:
+        copy.wait()
 
     lane = lax.broadcasted_iota(jnp.int32, (8, 128), 1)
     line = lax.broadcasted_iota(jnp.int32, (8, 128), 0)
@@ -299,35 +332,66 @@
         over(1, X + 1, tables)
     with jax.named_scope("forward_inside"):
         over(2, X, forward)
-    def forward_rows():
+        @pl.when(asks["x", 1])
+        def _():
+            wait_answer(("x", 1))
+            x_state[0]((1,))
+
+        @pl.when(asks["x", 0] & begins)
+        def _():
+            wait_answer(("x", 0))
+            x_state[0]((0,))
+
+        @pl.when(mutual["x", 0])
+        def _():
+            pl.semaphore_wait(barrier, 1)
+            x_state[0]((0,))
+
+    def by_sides(body, upper_first):
+        pl.when(upper_first)(lambda: body(1, X))
+        body(0, 1)
+        pl.when(jnp.logical_not(upper_first))(lambda: body(1, X))
+
+    def pack(buffer, *refs):
+        for side, row in ((0, 0), (1, Y - 1)):
+            for k, (ref, layer) in enumerate(corners(*refs)):
+                buffer[side, k:k + 1] = ref[layer, row:row + 1]
+
+    def unpack(buffer, *refs):
+        for side, aside in ((0, 0), (1, 7)):
+            @pl.when(has["y", side])
+            def _():
+                for k, (ref, layer) in enumerate(corners(*refs)):
+                    ref[layer, aside:aside + 1] = buffer[side, k:k + 1]
+
+    def forward_edge(side, layer):
+        x_state[1]((side,))
+        forward(layer)
+        by_rows(lambda act: act(layer), forward_row)
+        x_middle[0]((side,))
+
+    def backward_edge(side, layer):
+        x_middle[1]((side,))
+        backward(layer)
+        by_rows(lambda act: act(layer), backward_row)
+        x_last[0]((side,))
+
+    with jax.named_scope("forward_edges"):
+        y_state[1]()
+        by_sides(forward_edge, begins)
+        pack(CO, P1, M1, U1, V1)
+        y_edge[0]()
+    with jax.named_scope("forward_rows"):
         inside_rows(forward_row)
         y_middle[0]()
-
-    y_state[1]()
-    with jax.named_scope("forward_edges"):
-        x_state[1]()
-        edges(forward)
-        edge_rows(forward_row)
-        x_middle[0]()
-        for side, row in ((0, 0), (1, Y - 1)):
-            for k, (ref, layer) in enumerate(corners(P1, M1, U1, V1)):
-                CO[side, k:k + 1] = ref[layer, row:row + 1]
-        y_edge[0]()
-    with jax.named_scope("forward_rows_late"):
-        forward_rows()
     with jax.named_scope("backward_inside"):
         over(2, X, backward)
     with jax.named_scope("backward_edges"):
         y_edge[1]()
-        for side, aside in ((0, 0), (1, 7)):
-            @pl.when(has["y", side])
-            def _():
-                for k, (ref, layer) in enumerate(corners(HP1, HM1, HU1, HV1)):
-                    ref[layer, aside:aside + 1] = CI[side, k:k + 1]
-        x_middle[1]()
-        edges(backward)
-        edge_rows(backward_row)
-        x_last[0]()
+        unpack(CI, HP1, HM1, HU1, HV1)
+        by_sides(backward_edge, begins | ends)
+        pack(DO, U0, V0)
+        y_last_edge[0]()
     with jax.named_scope("backward_rows"):
         y_middle[1]()
         inside_rows(backward_row)
@@ -336,16 +400,21 @@
         over(2, X, finish)
         finish(1, below=False)
         finish(X, above=False)
+        for step in (x_state, y_state, x_middle, y_edge, y_middle):
+            step[2]()
     with jax.named_scope("finish_rows"):
         y_last[1]()
-        by_rows(lambda act: over(1, X + 1, act, 4), finish_row)
+        inside_rows(finish_row)
+        y_last_edge[1]()
+        unpack(DI, HU0, HV0)
+        edge_rows(finish_row)
     with jax.named_scope("finish_edges"):
         x_last[1]()
         for x, layer in ((0, 0), (X - 1, X + 1)):
             out_p[x] = out_p[x] + U0[layer]
             out_m[x] = out_m[x] + V0[layer]
     with jax.named_scope("wait_sends"):
-        for step in (x_state, y_state, x_middle, y_edge, y_middle, x_last, y_last):
+        for step in (x_last, y_last, y_last_edge):
             step[2]()
 
 
@@ -366,7 +435,7 @@
         f32, i32 = jnp.float32, jnp.int32
         hbm = pl.BlockSpec(memory_space=pltpu.HBM)
         vmem = pltpu.VMEM
-        copies = 2 * (2 + 4 + 2) + 2 * (2 + 1 + 4 + 2)
+        copies = 2 * (2 + 4 + 2) + 2 * (2 + 1 + 4 + 2 + 1)
         results = pl.pallas_call(
             functools.partial(kernel, nx_dev, ny_dev),
             out_shape=[vmem((X, Y, Z), f32)] * 2,
@@ -376,12 +445,13 @@
                 [vmem((X + 2, Y, Z), f32)] * 2
                 + [vmem((X + 2, Y, Z), i32)] * 3
                 + [vmem((X + 2, Y, Z), f32)] * 8
-                + [vmem((2, 8, Z), f32)] * 2
+                + [vmem((2, 8, Z), f32)] * 4
                 + [vmem((X + 2, 8, Z), f32)] * 8
                 + [vmem((X + 2, Y, Z), f32)] * 13
                 + [pltpu.SMEM(args[7].shape, f32), pltpu.SMEM(args[8].shape, f32)]
                 + [pltpu.SemaphoreType.DMA((9,))]
                 + [pltpu.SemaphoreType.DMA((copies,))] * 2
+                + [pltpu.SemaphoreType.REGULAR((4,))]
             ),
             compiler_params=pltpu.CompilerParams(
                 collective_id=0, has_side_effects=True, vmem_limit_bytes=32 * 1024 * 1024

time: 24.4 us -> 23.9 us (0.980)
  the two profiles are of different devices: /device:TPU:23 before, /device:TPU:34 now
where the time goes in v6:
time: 23.9 us; the launch traced here: 23.6 us
  Pallas kernels  22.9 us (96%)
  between operations  0.64 us (3%)
    pallas_call x1, Pallas kernels, on_device(): pl.pallas_call(functools.partial(kernel, nx_dev, ny_dev), out_shape=[vmem...  22 us
    pallas_call x1, Pallas kernels, on_device(): pl.pallas_call(hand_over, out_shape=[jax.ShapeDtypeStruct((X, Y, Z), f32)...  0.89 us

profile of v6, /device:TPU:34, one launch (start us, length us, event | category | flops | bytes accessed | tf_op | source)
XLA Modules:
  0.0 23.6 jit_solution(18284969430836135744)
XLA Ops:
  0.6 22.0 %reverse.1 = (f32[24,16,256]{2,1,0:T(8,128)S(1)}, f32[24,16,256]{2,1,0:T(8,128)S(1)}) custom-call(f32[24,16,256]{2,1,0:T(8,128)} %p_hbm.1, f32[24,16,256]{2,1,0:T(8,128)} %m_hbm.1, f32[24,16,256]{2,1,0:T(8,128)} %a_hbm.1, f32[24,16,256]{2,1,0:T(8,128)} %b_hbm.1, s32[24,16,256]{2,1,0:T(8,128)} %or_hbm.1, s32[24,16,256]{2,1,0:T(8,128)} %an_hbm.1, ...), custom_call_target="tpu_custom_call" | custom-call | tf_op jit(solution)/shard_map/reverse/pallas_call | solution.py:439
  22.7 0.9 %hand_over.1 = (f32[24,16,256]{2,1,0:T(8,128)}, f32[24,16,256]{2,1,0:T(8,128)}) custom-call(f32[24,16,256]{2,1,0:T(8,128)S(1)} %get-tuple-element.4.p_ref, f32[24,16,256]{2,1,0:T(8,128)S(1)} %get-tuple-element.5.m_ref), custom_call_target="tpu_custom_call" | custom-call | tf_op jit(solution)/shard_map/hand_over/pallas_call | solution.py:462

commit v7 on v6

--- a/solution.py
+++ b/solution.py
@@ -43,11 +43,15 @@
     nx_dev, ny_dev,
     p_hbm, m_hbm, a_hbm, b_hbm, or_hbm, an_hbm, bm_hbm, st_hbm, pt_hbm,
     out_p, out_m,
-    A, B, OR, AN, BM, P0, M0, P1, M1, U1, V1, U0, V0, CO, CI, DO, DI, HP0, HM0, HP1, HM1, HU1, HV1, HU0, HV0,
+    A, B, OR, AN, BM, S0, S1, S2, H0, H1, H2,
     KAP, JMP, MOV, REACH, JS0, JD0, W0, G0, K0, JS1, JD1, W1, SP1, st, pt,
     load_sem, ss, rs, ready,
 ):
     X, Y, Z = p_hbm.shape
+    P0, M0, HP0, HM0 = S0.at[:, 0], S0.at[:, 1], H0.at[:, 0], H0.at[:, 1]
+    P1, M1, U1, V1 = (S1.at[:, k] for k in range(4))
+    HP1, HM1, HU1, HV1 = (H1.at[:, k] for k in range(4))
+    U0, V0, HU0, HV0 = S2.at[:, 0], S2.at[:, 1], H2.at[:, 0], H2.at[:, 1]
     gx, gy = lax.axis_index("gx"), lax.axis_index("gy")
     has = {
         ("x", 0): gx > 0, ("x", 1): gx < nx_dev - 1,
@@ -84,7 +88,7 @@
     own = pl.ds(1, X)
     loads = []
     for k, (src, dst) in enumerate((
-        (p_hbm, P0.at[own]), (m_hbm, M0.at[own]),
+        (p_hbm, S0.at[own, 0]), (m_hbm, S0.at[own, 1]),
         (an_hbm, AN.at[own]), (or_hbm, OR.at[own]), (bm_hbm, BM.at[own]), (st_hbm, st), (pt_hbm, pt),
         (a_hbm, A.at[own]), (b_hbm, B.at[own]),
     )):
@@ -101,6 +105,8 @@
         arrivals = {0: [], 1: []}
         for down, down_to, up, up_to in pieces:
             for side, src, dst in ((0, down, down_to), (1, up, up_to)):
+                if src is None:
+                    continue
                 k = next(sems)
                 copy = pltpu.make_async_remote_copy(
                     src_ref=src, dst_ref=dst, send_sem=ss.at[k], recv_sem=rs.at[k],
@@ -130,24 +136,32 @@
     inside = pl.ds(2, X - 2)
 
     def y_faces(ref, aside, layers=own):
-        return ref.at[layers, 0], aside.at[layers, 7], ref.at[layers, Y - 1], aside.at[layers, 0]
+        return ref.at[layers, :, 0], aside.at[layers, :, 7], ref.at[layers, :, Y - 1], aside.at[layers, :, 0]
 
     x_state = exchange("x", [
-        (ref.at[1], ref.at[X + 1], src.at[X - 1], ref.at[0]) for src, ref in ((p_hbm, P0), (m_hbm, M0))
+        (S0.at[1], S0.at[X + 1], None, None),
+        (None, None, p_hbm.at[X - 1], S0.at[0, 0]),
+        (None, None, m_hbm.at[X - 1], S0.at[0, 1]),
     ])
-    y_state = exchange("y", [y_faces(P0, HP0), y_faces(M0, HM0)])
-    x_middle = exchange("x", [x_faces(ref) for ref in (P1, M1, U1, V1)])
-    y_edge = exchange("y", [(CO.at[0], CI.at[1], CO.at[1], CI.at[0])])
-    y_middle = exchange("y", [y_faces(P1, HP1, inside), y_faces(M1, HM1, inside), y_faces(U1, HU1, inside), y_faces(V1, HV1, inside)])
-    x_last = exchange("x", [x_faces(ref) for ref in (U0, V0)])
-    y_last = exchange("y", [y_faces(U0, HU0, inside), y_faces(V0, HV0, inside)])
-    y_last_edge = exchange("y", [(DO.at[0], DI.at[1], DO.at[1], DI.at[0])])
+    y_state = exchange("y", [y_faces(S0, H0)])
+    x_middle = exchange("x", [x_faces(S1)])
+    y_edge = [exchange("y", [y_faces(S1, H1, layer)]) for layer in (1, X)]
+    y_middle = exchange("y", [y_faces(S1, H1, inside)])
+    x_last = exchange("x", [x_faces(S2)])
+    y_last = exchange("y", [y_faces(S2, H2, inside)])
+    y_last_edge = [exchange("y", [y_faces(S2, H2, layer)]) for layer in (1, X)]
 
     for side, layer in enumerate((0, X + 1)):
         @pl.when(jnp.logical_not(has["x", side]))
         def _():
-            for ref in (P0, M0, P1, M1, U1, V1, U0, V0):
-                ref[layer] = jnp.zeros((Y, Z), ref.dtype)
+            for ref in (S0, S1, S2):
+                ref[layer] = jnp.zeros(ref.shape[1:], ref.dtype)
+    for side, row in ((0, 0), (1, 7)):
+        @pl.when(jnp.logical_not(has["y", side]))
+        def _():
+            for ref in (H0, H1):
+                for layer in (1, X):
+                    ref[layer, :, row:row + 1] = jnp.zeros((ref.shape[1], 1, Z), ref.dtype)
 
     pl.when(count > 0)(lambda: pl.semaphore_wait(barrier, count))
     for axis, side in has:
@@ -184,7 +198,7 @@
         turned = [pltpu.roll(part, by % size, axis) for part in parts]
         return [jnp.where(edge, before, here) for before, here in zip([0.0] + turned, turned)]
 
-    def lap(ref, i, below=True, above=True):
+    def lap(ref, i, below=True, above=True, aside=None):
         tiles = [[ref[i, a:a + 8, b:b + 128] for b in range(0, Z, 128)] for a in range(0, Y, 8)]
         result = []
         along_y = []
@@ -192,6 +206,11 @@
             down = shifted(column, 1, 8, 0, first_line)
             up = shifted(column[::-1], -1, 8, 0, last_line)[::-1]
             along_y.append([d + u for d, u in zip(down, up)])
+        if aside is not None:
+            for b, column in enumerate(along_y):
+                beyond = aside[i, :, 128 * b:128 * (b + 1)]
+                column[0] = column[0] + jnp.where(first_line, beyond, 0.0)
+                column[-1] = column[-1] + jnp.where(last_line, beyond, 0.0)
         for a, row in enumerate(tiles):
             left = shifted(row, 1, 128, 1, first_lane)
             right = shifted(row[::-1], -1, 128, 1, last_lane)[::-1]
@@ -219,19 +238,19 @@
         U1[at] = KAP[at] * (REACH[at] * (A[at] - spread * (jump * slope)))
         V1[at] = diffusion_step * spread
 
-    def forward(i):
+    def forward(i, aside=(None, None)):
         phase, potential = P0[i], M0[i]
         jump = JMP[i]
         t, slope, slope_derivative, release = local_terms(phase, jump)
         held_slope, held_derivative = jump * slope, jump * slope_derivative
         drive = (
-            KAP[i] * lap(P0, i)
+            KAP[i] * lap(P0, i, aside=aside[0])
             - 2.0 * well_height * t * (1.0 - 2.0 * phase)
             + coupling * held_slope * potential
         )
         step = REACH[i] * drive
         yielding = MOV[i] * release
-        flux = yielding * (diffusion_step * lap(M0, i) - held_slope * step)
+        flux = yielding * (diffusion_step * lap(M0, i, aside=aside[1]) - held_slope * step)
         P1[i] = phase + step
         M1[i] = potential + flux
         JS0[i] = held_slope
@@ -251,20 +270,20 @@
         K0[here] = K0[here] + JS0[here] * flux - JD0[here] * step
         sensitivities(here, phase)
 
-    def backward(i):
+    def backward(i, aside=(None, None, None, None)):
         x = i - 1
         phase, potential = P1[i], M1[i]
         jump, reach = JMP[i], REACH[i]
         t, slope, slope_derivative, release = local_terms(phase, jump)
         held_slope, held_derivative = jump * slope, jump * slope_derivative
         drive = (
-            KAP[i] * lap(P1, i)
+            KAP[i] * lap(P1, i, aside=aside[0])
             - 2.0 * well_height * t * (1.0 - 2.0 * phase)
             + coupling * held_slope * potential
         )
         step = reach * drive
         yielding = MOV[i] * release
-        flux = yielding * (diffusion_step * lap(M1, i) - held_slope * step)
+        flux = yielding * (diffusion_step * lap(M1, i, aside=aside[1]) - held_slope * step)
         gain = well_height * (12.0 * t - 2.0) + coupling * held_derivative * potential
         keep = held_slope * flux - held_derivative * step
         spread = B[i] * yielding
@@ -273,8 +292,8 @@
         JD1[i] = held_derivative
         W1[i] = yielding
         SP1[i] = spread
-        bar_p = A[i] + pull * gain + spread * keep + lap(U1, i)
-        bar_m = B[i] + coupling * held_slope * pull + lap(V1, i)
+        bar_p = A[i] + pull * gain + spread * keep + lap(U1, i, aside=aside[2])
+        bar_m = B[i] + coupling * held_slope * pull + lap(V1, i, aside=aside[3])
         spread = bar_m * W0[i]
         pull = reach * (bar_p - spread * JS0[i])
         U0[i] = KAP[i] * pull
@@ -325,9 +344,6 @@
     def edge_rows(body):
         by_rows(edges, body)
 
-    def corners(*refs):
-        return [(ref, layer) for ref in refs for layer in (1, X)]
-
     with jax.named_scope("tables"):
         over(1, X + 1, tables)
     with jax.named_scope("forward_inside"):
@@ -347,66 +363,61 @@
             pl.semaphore_wait(barrier, 1)
             x_state[0]((0,))
 
-    def by_sides(body, upper_first):
+    def by_sides(body, upper_first, between=None):
+        def do_between(order):
+            if between is not None:
+                pl.when(order & between[1])(between[0])
+
+        lower_first = jnp.logical_not(upper_first)
         pl.when(upper_first)(lambda: body(1, X))
+        do_between(upper_first)
         body(0, 1)
-        pl.when(jnp.logical_not(upper_first))(lambda: body(1, X))
-
-    def pack(buffer, *refs):
-        for side, row in ((0, 0), (1, Y - 1)):
-            for k, (ref, layer) in enumerate(corners(*refs)):
-                buffer[side, k:k + 1] = ref[layer, row:row + 1]
-
-    def unpack(buffer, *refs):
-        for side, aside in ((0, 0), (1, 7)):
-            @pl.when(has["y", side])
-            def _():
-                for k, (ref, layer) in enumerate(corners(*refs)):
-                    ref[layer, aside:aside + 1] = buffer[side, k:k + 1]
+        do_between(lower_first)
+        pl.when(lower_first)(lambda: body(1, X))
 
     def forward_edge(side, layer):
         x_state[1]((side,))
-        forward(layer)
-        by_rows(lambda act: act(layer), forward_row)
+        forward(layer, (HP0, HM0))
         x_middle[0]((side,))
+        y_edge[side][0]()
 
     def backward_edge(side, layer):
+        y_edge[side][1]()
         x_middle[1]((side,))
-        backward(layer)
-        by_rows(lambda act: act(layer), backward_row)
+        backward(layer, (HP1, HM1, HU1, HV1))
         x_last[0]((side,))
+        y_last_edge[side][0]()
+
+    def backward_rows():
+        y_middle[1]()
+        inside_rows(backward_row)
+        y_last[0]()
+
+    rows_between = at < 2
 
     with jax.named_scope("forward_edges"):
         y_state[1]()
         by_sides(forward_edge, begins)
-        pack(CO, P1, M1, U1, V1)
-        y_edge[0]()
     with jax.named_scope("forward_rows"):
         inside_rows(forward_row)
         y_middle[0]()
     with jax.named_scope("backward_inside"):
         over(2, X, backward)
     with jax.named_scope("backward_edges"):
-        y_edge[1]()
-        unpack(CI, HP1, HM1, HU1, HV1)
-        by_sides(backward_edge, begins | ends)
-        pack(DO, U0, V0)
-        y_last_edge[0]()
+        by_sides(backward_edge, begins | ends, (backward_rows, rows_between))
     with jax.named_scope("backward_rows"):
-        y_middle[1]()
-        inside_rows(backward_row)
-        y_last[0]()
+        pl.when(jnp.logical_not(rows_between))(backward_rows)
     with jax.named_scope("finish_inside"):
         over(2, X, finish)
         finish(1, below=False)
         finish(X, above=False)
-        for step in (x_state, y_state, x_middle, y_edge, y_middle):
+        for step in (x_state, y_state, x_middle, *y_edge, y_middle):
             step[2]()
     with jax.named_scope("finish_rows"):
         y_last[1]()
         inside_rows(finish_row)
-        y_last_edge[1]()
-        unpack(DI, HU0, HV0)
+        for edge in y_last_edge:
+            edge[1]()
         edge_rows(finish_row)
     with jax.named_scope("finish_edges"):
         x_last[1]()
@@ -414,7 +425,7 @@
             out_p[x] = out_p[x] + U0[layer]
             out_m[x] = out_m[x] + V0[layer]
     with jax.named_scope("wait_sends"):
-        for step in (x_last, y_last, y_last_edge):
+        for step in (x_last, y_last, *y_last_edge):
             step[2]()
 
 
@@ -435,7 +446,7 @@
         f32, i32 = jnp.float32, jnp.int32
         hbm = pl.BlockSpec(memory_space=pltpu.HBM)
         vmem = pltpu.VMEM
-        copies = 2 * (2 + 4 + 2) + 2 * (2 + 1 + 4 + 2 + 1)
+        copies = 4 + 2 * 9
         results = pl.pallas_call(
             functools.partial(kernel, nx_dev, ny_dev),
             out_shape=[vmem((X, Y, Z), f32)] * 2,
@@ -444,9 +455,8 @@
             scratch_shapes=(
                 [vmem((X + 2, Y, Z), f32)] * 2
                 + [vmem((X + 2, Y, Z), i32)] * 3
-                + [vmem((X + 2, Y, Z), f32)] * 8
-                + [vmem((2, 8, Z), f32)] * 4
-                + [vmem((X + 2, 8, Z), f32)] * 8
+                + [vmem((X + 2, k, Y, Z), f32) for k in (2, 4, 2)]
+                + [vmem((X + 2, k, 8, Z), f32) for k in (2, 4, 2)]
                 + [vmem((X + 2, Y, Z), f32)] * 13
                 + [pltpu.SMEM(args[7].shape, f32), pltpu.SMEM(args[8].shape, f32)]
                 + [pltpu.SemaphoreType.DMA((9,))]

time: 23.9 us -> 23.2 us (0.971)
  the two profiles are of different devices: /device:TPU:34 before, /device:TPU:38 now
where the time goes in v7:
time: 23.2 us; the launch traced here: 23 us
  Pallas kernels  22.4 us (97%)
  between operations  0.64 us (3%)
    pallas_call x1, Pallas kernels, on_device(): pl.pallas_call(functools.partial(kernel, nx_dev, ny_dev), out_shape=[vmem...  21.5 us
    pallas_call x1, Pallas kernels, on_device(): pl.pallas_call(hand_over, out_shape=[jax.ShapeDtypeStruct((X, Y, Z), f32)...  0.89 us

profile of v7, /device:TPU:38, one launch (start us, length us, event | category | flops | bytes accessed | tf_op | source)
XLA Modules:
  0.0 23.0 jit_solution(8450399129562726893)
XLA Ops:
  0.6 21.5 %reverse.1 = (f32[24,16,256]{2,1,0:T(8,128)S(1)}, f32[24,16,256]{2,1,0:T(8,128)S(1)}) custom-call(f32[24,16,256]{2,1,0:T(8,128)} %p_hbm.1, f32[24,16,256]{2,1,0:T(8,128)} %m_hbm.1, f32[24,16,256]{2,1,0:T(8,128)} %a_hbm.1, f32[24,16,256]{2,1,0:T(8,128)} %b_hbm.1, s32[24,16,256]{2,1,0:T(8,128)} %or_hbm.1, s32[24,16,256]{2,1,0:T(8,128)} %an_hbm.1, ...), custom_call_target="tpu_custom_call" | custom-call | tf_op jit(solution)/shard_map/reverse/pallas_call | solution.py:450
  22.1 0.9 %hand_over.1 = (f32[24,16,256]{2,1,0:T(8,128)}, f32[24,16,256]{2,1,0:T(8,128)}) custom-call(f32[24,16,256]{2,1,0:T(8,128)S(1)} %get-tuple-element.4.p_ref, f32[24,16,256]{2,1,0:T(8,128)S(1)} %get-tuple-element.5.m_ref), custom_call_target="tpu_custom_call" | custom-call | tf_op jit(solution)/shard_map/hand_over/pallas_call | solution.py:472

commit v8 on v7

--- a/solution.py
+++ b/solution.py
@@ -375,10 +375,13 @@
         do_between(lower_first)
         pl.when(lower_first)(lambda: body(1, X))
 
+    after = (gy >= ny_dev // 2) | odd
+    let_go = {0: begins & after, 1: ends & after}
+
     def forward_edge(side, layer):
         x_state[1]((side,))
         forward(layer, (HP0, HM0))
-        x_middle[0]((side,))
+        pl.when(jnp.logical_not(let_go[side]))(lambda: x_middle[0]((side,)))
         y_edge[side][0]()
 
     def backward_edge(side, layer):
@@ -400,9 +403,13 @@
         by_sides(forward_edge, begins)
     with jax.named_scope("forward_rows"):
         inside_rows(forward_row)
-        y_middle[0]()
+        for side in (0, 1):
+            pl.when(let_go[side])(lambda: x_middle[0]((side,)))
+        rows_later = ends & ((gy == ny_dev // 2 - 1) | (gy == ny_dev // 2))
+        pl.when(jnp.logical_not(rows_later))(lambda: y_middle[0]())
     with jax.named_scope("backward_inside"):
         over(2, X, backward)
+        pl.when(rows_later)(lambda: y_middle[0]())
     with jax.named_scope("backward_edges"):
         by_sides(backward_edge, begins | ends, (backward_rows, rows_between))
     with jax.named_scope("backward_rows"):

time: 23.2 us -> 22.5 us (0.970)
  the two profiles are of different devices: /device:TPU:38 before, /device:TPU:34 now
where the time goes in v8:
time: 22.5 us; the launch traced here: 22.1 us
  Pallas kernels  21.5 us (96%)
  between operations  0.64 us (3%)
    pallas_call x1, Pallas kernels, on_device(): pl.pallas_call(functools.partial(kernel, nx_dev, ny_dev), out_shape=[vmem...  20.6 us
    pallas_call x1, Pallas kernels, on_device(): pl.pallas_call(hand_over, out_shape=[jax.ShapeDtypeStruct((X, Y, Z), f32)...  0.89 us

profile of v8, /device:TPU:34, one launch (start us, length us, event | category | flops | bytes accessed | tf_op | source)
XLA Modules:
  0.0 22.1 jit_solution(3676378566894845861)
XLA Ops:
  0.6 20.6 %reverse.1 = (f32[24,16,256]{2,1,0:T(8,128)S(1)}, f32[24,16,256]{2,1,0:T(8,128)S(1)}) custom-call(f32[24,16,256]{2,1,0:T(8,128)} %p_hbm.1, f32[24,16,256]{2,1,0:T(8,128)} %m_hbm.1, f32[24,16,256]{2,1,0:T(8,128)} %a_hbm.1, f32[24,16,256]{2,1,0:T(8,128)} %b_hbm.1, s32[24,16,256]{2,1,0:T(8,128)} %or_hbm.1, s32[24,16,256]{2,1,0:T(8,128)} %an_hbm.1, ...), custom_call_target="tpu_custom_call" | custom-call | tf_op jit(solution)/shard_map/reverse/pallas_call | solution.py:457
  21.2 0.9 %hand_over.1 = (f32[24,16,256]{2,1,0:T(8,128)}, f32[24,16,256]{2,1,0:T(8,128)}) custom-call(f32[24,16,256]{2,1,0:T(8,128)S(1)} %get-tuple-element.4.p_ref, f32[24,16,256]{2,1,0:T(8,128)S(1)} %get-tuple-element.5.m_ref), custom_call_target="tpu_custom_call" | custom-call | tf_op jit(solution)/shard_map/hand_over/pallas_call | solution.py:479

commit v9 on v8

--- a/solution.py
+++ b/solution.py
@@ -65,10 +65,12 @@
     at, even = lax.rem(gx, RUN), lax.rem(gy, 2) == 0
     odd, begins, ends = jnp.logical_not(even), at == 0, at == RUN - 1
     mutual = {("x", 0): has["x", 0] & begins & odd, ("x", 1): has["x", 1] & ends & odd}
-    caller = begins ^ even
+    half = ny_dev // 2
+    calls_down = (begins & odd) | (jnp.logical_not(begins) & (gy == half))
+    calls_up = (begins & odd) | (jnp.logical_not(begins) & (gy != half - 1))
     calls = {
         ("x", 0): has["x", 0] & (begins | ends), ("x", 1): (has["x", 1] & (at < 2)) | mutual["x", 1],
-        ("y", 0): has["y", 0] & caller, ("y", 1): has["y", 1] & caller,
+        ("y", 0): has["y", 0] & calls_down, ("y", 1): has["y", 1] & calls_up,
     }
     called = {key: has[key] & jnp.logical_not(calls[key]) for key in has}
     asks = dict(calls)
@@ -375,8 +377,8 @@
         do_between(lower_first)
         pl.when(lower_first)(lambda: body(1, X))
 
-    after = (gy >= ny_dev // 2) | odd
-    let_go = {0: begins & after, 1: ends & after}
+    after = (gy >= half) | odd
+    let_go = {0: begins & (gy >= half), 1: ends & after}
 
     def forward_edge(side, layer):
         x_state[1]((side,))
@@ -398,15 +400,21 @@
 
     rows_between = at < 2
 
+    middle = (gy == half - 1) | (gy == half)
+    rows_later = ends & middle
+    rows_early = begins & (jnp.logical_not(after) | middle)
+
+    def forward_rows():
+        inside_rows(forward_row)
+        pl.when(jnp.logical_not(rows_later))(lambda: y_middle[0]())
+
     with jax.named_scope("forward_edges"):
         y_state[1]()
-        by_sides(forward_edge, begins)
+        by_sides(forward_edge, begins, (forward_rows, rows_early))
     with jax.named_scope("forward_rows"):
-        inside_rows(forward_row)
+        pl.when(jnp.logical_not(rows_early))(forward_rows)
         for side in (0, 1):
             pl.when(let_go[side])(lambda: x_middle[0]((side,)))
-        rows_later = ends & ((gy == ny_dev // 2 - 1) | (gy == ny_dev // 2))
-        pl.when(jnp.logical_not(rows_later))(lambda: y_middle[0]())
     with jax.named_scope("backward_inside"):
         over(2, X, backward)
         pl.when(rows_later)(lambda: y_middle[0]())

time: 22.5 us -> 22.5 us (level)
  the two profiles are of different devices: /device:TPU:34 before, /device:TPU:160 now
where the time goes in v9:
time: 22.5 us; the launch traced here: 22.4 us
  Pallas kernels  21.8 us (97%)
  between operations  0.64 us (3%)
    pallas_call x1, Pallas kernels, on_device(): pl.pallas_call(functools.partial(kernel, nx_dev, ny_dev), out_shape=[vmem...  20.9 us
    pallas_call x1, Pallas kernels, on_device(): pl.pallas_call(hand_over, out_shape=[jax.ShapeDtypeStruct((X, Y, Z), f32)...  0.89 us

profile of v9, /device:TPU:160, one launch (start us, length us, event | category | flops | bytes accessed | tf_op | source)
XLA Modules:
  0.0 22.4 jit_solution(3744530734872862946)
XLA Ops:
  0.6 20.9 %reverse.1 = (f32[24,16,256]{2,1,0:T(8,128)S(1)}, f32[24,16,256]{2,1,0:T(8,128)S(1)}) custom-call(f32[24,16,256]{2,1,0:T(8,128)} %p_hbm.1, f32[24,16,256]{2,1,0:T(8,128)} %m_hbm.1, f32[24,16,256]{2,1,0:T(8,128)} %a_hbm.1, f32[24,16,256]{2,1,0:T(8,128)} %b_hbm.1, s32[24,16,256]{2,1,0:T(8,128)} %or_hbm.1, s32[24,16,256]{2,1,0:T(8,128)} %an_hbm.1, ...), custom_call_target="tpu_custom_call" | custom-call | tf_op jit(solution)/shard_map/reverse/pallas_call | solution.py:465
  21.5 0.9 %hand_over.1 = (f32[24,16,256]{2,1,0:T(8,128)}, f32[24,16,256]{2,1,0:T(8,128)}) custom-call(f32[24,16,256]{2,1,0:T(8,128)S(1)} %get-tuple-element.4.p_ref, f32[24,16,256]{2,1,0:T(8,128)S(1)} %get-tuple-element.5.m_ref), custom_call_target="tpu_custom_call" | custom-call | tf_op jit(solution)/shard_map/hand_over/pallas_call | solution.py:487
